TPU v7x, 32 devices: a whole 2x2x4 slice. The times are simulated.
32 devices in a mesh: rep: 2 (over x), dp: 4 (over z), tp: 4 (over y, core).
Axes of the slice: x: 2, y: 2, z: 4, core: 2. Of those that a mesh axis runs over, the one named last changes fastest.
Arguments:
- attention_output: bfloat16 [4, 1024, 8192], P(None, ('rep', 'dp'), 'tp'), parts along dimension 1, may hold values from -6 to 6
- output_projection_weight: bfloat16 [8192, 8192], P('tp'), may hold values from -0.09375 to 0.09375
- shrink_matrix_store: bfloat16 [256, 16, 8192], P('dp', None, 'tp'), may hold values from -0.0625 to 0.0625
- expand_matrix_store: bfloat16 [256, 16, 8192], P('dp', None, 'tp'), may hold values from -1.5 to 1.5
- segment_adapter: int32 [4, 64], P(None, ('rep', 'dp')), parts along dimension 1, may hold values from 0 to 255, as said below
- segment_live_rows: int32 [4, 64], P(None, ('rep', 'dp')), parts along dimension 1, may hold values from 1 to 16, as said below
- adapter_store_index: int32 [512], P('rep'), parts along dimension 0, may hold values from 0 to 255, as said below
Outputs:
- projected: bfloat16 [4, 1024, 8192], P(None, ('rep', 'dp'), 'tp'), parts along dimension 1
There are 2 independent parts, one for each index of `rep`. A program takes and returns all parts, laid end to end along the dimension named above; an argument that names none is the same for every part. Nothing has to cross between parts.
Inputs may be any that keep to these rules, and one draw needn't show every extreme that they name: `segment_adapter`: adapter stored at position p lies on index p // 64 of dp. Over all 4 steps, the segments of one index of dp name adapters of which at most 16 lie on any one index of dp, and exactly 16 lie on one of them. `segment_live_rows`: every step of every index of dp has a segment with all 16 rows live. `adapter_store_index`: A permutation: each store position holds one adapter.
All inputs are finite; a program needn't handle non-finite values.
Results may differ from a plain program's by a relative error of at most 0.0095.
Values may be sent and summed in bfloat16 or wider, within the bound.
No kernel may reach another device: no remote copies, remote signals or barrier semaphores. Data moves between devices by JAX's collectives and lax.ppermute only.
A program may use at most 192 MiB of HBM per device.

v0:
```python
import jax
import jax.numpy as jnp
from jax import lax
from jax.sharding import PartitionSpec as P


def per_device(
    attention_output,
    output_projection_weight,
    shrink_matrix_store,
    expand_matrix_store,
    segment_adapter,
    segment_live_rows,
    adapter_store_index,
):
    steps_count, rows_dev, width_dev = attention_output.shape
    seg_count = segment_adapter.shape[1]
    seg_len = rows_dev // seg_count
    adapter_rank_width = shrink_matrix_store.shape[1]
    store_portion = shrink_matrix_store.shape[0]
    flat_ids = segment_adapter.reshape(-1)
    count = flat_ids.shape[0]
    table_ids = jnp.arange(adapter_store_index.shape[0], dtype=jnp.int32)
    positions = jnp.sum(
        jnp.where(flat_ids[:, None] == table_ids[None, :], adapter_store_index[None, :], 0), axis=1
    )
    owners = positions // store_portion
    local_slot = positions % store_portion
    n_owners = lax.axis_size("dp")
    capacity = count // 2
    order_ids = jnp.arange(count, dtype=jnp.int32)
    same_owner = owners[:, None] == owners[None, :]
    earlier = order_ids[:, None] > order_ids[None, :]
    ranks = jnp.sum(jnp.where(same_owner & earlier, 1, 0), axis=1).astype(jnp.int32)
    owner_match = owners[:, None] == jnp.arange(n_owners, dtype=jnp.int32)[None, :]
    rank_match = ranks[:, None] == jnp.arange(capacity, dtype=jnp.int32)[None, :]
    requests = jnp.sum(
        jnp.where(owner_match[:, :, None] & rank_match[:, None, :], local_slot[:, None, None], 0),
        axis=0,
    )
    requested_adapter = lax.all_to_all(requests, "dp", split_axis=0, concat_axis=0, tiled=True)
    located_shrink = shrink_matrix_store[requested_adapter]
    located_expand = expand_matrix_store[requested_adapter]
    got_a = lax.all_to_all(located_shrink, "dp", split_axis=0, concat_axis=0, tiled=True)
    got_b = lax.all_to_all(located_expand, "dp", split_axis=0, concat_axis=0, tiled=True)
    pick = owners * capacity + ranks
    selected_shrink = got_a.reshape(n_owners * capacity, adapter_rank_width, width_dev)[pick]
    selected_expand = got_b.reshape(n_owners * capacity, adapter_rank_width, width_dev)[pick]
    selected_shrink = selected_shrink.reshape(steps_count, seg_count, adapter_rank_width, width_dev)
    selected_expand = selected_expand.reshape(steps_count, seg_count, adapter_rank_width, width_dev)
    grouped = attention_output.reshape(steps_count, seg_count, seg_len, width_dev)
    live = (
        jnp.arange(seg_len, dtype=jnp.int32)[None, None, :] < segment_live_rows[:, :, None]
    ).astype(jnp.float32)
    shrink_part = jnp.einsum(
        "tgsd,tgrd->tgsr", grouped, selected_shrink, preferred_element_type=jnp.float32
    )
    shrink_part = shrink_part * live[:, :, :, None]
    results = []
    for decode_step_index in range(steps_count):
        base_part = jnp.dot(
            attention_output[decode_step_index],
            output_projection_weight,
            preferred_element_type=jnp.float32,
        )
        base = lax.psum_scatter(
            base_part.astype(jnp.bfloat16), "tp", scatter_dimension=1, tiled=True
        ).astype(jnp.float32)
        shrink_now = lax.psum(shrink_part[decode_step_index], "tp")
        delta = jnp.einsum(
            "gsr,grd->gsd",
            shrink_now,
            selected_expand[decode_step_index].astype(jnp.float32),
            precision=lax.Precision.HIGHEST,
        )
        results.append((base + delta.reshape(rows_dev, width_dev)).astype(jnp.bfloat16))
    return jnp.stack(results)


def solution(mesh):
    return jax.shard_map(
        per_device,
        mesh=mesh,
        in_specs=(
            P(None, ("rep", "dp"), "tp"),
            P("tp", None),
            P("dp", None, "tp"),
            P("dp", None, "tp"),
            P(None, ("rep", "dp")),
            P(None, ("rep", "dp")),
            P("rep"),
        ),
        out_specs=P(None, ("rep", "dp"), "tp"),
        check_vma=False,
    )
```

profile of v0, /device:TPU:0, one launch (start us, length us, event | category | flops | bytes accessed | tf_op | source)
XLA Modules:
  0.0 274.3 jit_solution(14777361461436571210)
XLA Ops:
  6.5 0.8 eq.64
  7.3 0.9 select_reduce_fusion.1
  8.2 0.2 select_reduce_fusion.2
  8.4 0.7 select_reduce_fusion
  9.1 6.3 %all-to-all-start = ((s32[4,1,16]{2,1,0:T(1,128)}), s32[4,1,16]{2,1,0:T(1,128)S(1)}, u32[]{:S(2)}, u32[]{:S(2)}) async-start(s32[4,1,16]{2,1,0:T(1,128)} %bitcast.2), calls=%async_computation.1 | async-start | bytes 4096 | tf_op jit(solution)/shard_map/all_to_all | solution.py:41
  15.4 16.6 %convolution_convert_fusion.3 = bf16[128,8192]{1,0:T(8,128)(2,1)} fusion(bf16[2048,8192]{1,0:T(8,128)(2,1)} %param.8, bf16[4,128,2048]{2,1,0:T(8,128)(2,1)} %param.7), kind=kOutput, calls=%fused_computation.7 | convolution fusion | flops 4296015872 | bytes 36175872 | tf_op jit(solution)/shard_map/dot_general | solution.py:61
  32.1 0.1 reshape.217
  32.1 5.0 %gather_fusion = bf16[64,16,2048]{2,1,0:T(8,128)(2,1)} fusion(bf16[64,16,2048]{2,1,0:T(8,128)(2,1)} %param.9, s32[1024]{0:T(1024)S(1)} %pad_clamp_fusion.1), kind=kCustom, calls=%fused_computation | custom fusion | bytes 8388864 | tf_op jit(solution)/shard_map/gather | solution.py:42
  37.1 5.2 %all-to-all-start.1 = ((bf16[4,16,16,2048]{3,2,1,0:T(8,128)(2,1)}), bf16[4,16,16,2048]{3,2,1,0:T(8,128)(2,1)}, u32[]{:S(2)}, u32[]{:S(2)}) async-start(bf16[4,16,16,2048]{3,2,1,0:T(8,128)(2,1)} %bitcast.81), calls=%async_computation.2 | async-start | bytes 8388608 | tf_op jit(solution)/shard_map/all_to_all | solution.py:44
  42.4 16.8 %convolution_convert_fusion.2 = bf16[128,8192]{1,0:T(8,128)(2,1)} fusion(bf16[2048,8192]{1,0:T(8,128)(2,1)} %param.8, bf16[4,128,2048]{2,1,0:T(8,128)(2,1)S(1)} %copy-done), kind=kOutput, calls=%fused_computation.6 | convolution fusion | flops 4296015872 | bytes 36175872 | tf_op jit(solution)/shard_map/dot_general | solution.py:61
  59.2 5.0 %gather_fusion.2 = bf16[64,16,2048]{2,1,0:T(8,128)(2,1)} fusion(bf16[64,16,2048]{2,1,0:T(8,128)(2,1)} %param.10, s32[1024]{0:T(1024)S(1)} %pad_clamp_fusion.1), kind=kCustom, calls=%fused_computation.2 | custom fusion | bytes 8388864 | tf_op jit(solution)/shard_map/gather | solution.py:43
  64.2 71.2 %all-to-all-done.1 = bf16[4,16,16,2048]{3,2,1,0:T(8,128)(2,1)} async-done(((bf16[4,16,16,2048]{3,2,1,0:T(8,128)(2,1)}), bf16[4,16,16,2048]{3,2,1,0:T(8,128)(2,1)}, u32[]{:S(2)}, u32[]{:S(2)}) %all-to-all-start.1) | async-done | bytes 4194336 | tf_op jit(solution)/shard_map/all_to_all | solution.py:44
  135.4 4.8 %all-to-all-start.2 = ((bf16[4,16,16,2048]{3,2,1,0:T(8,128)(2,1)}), bf16[4,16,16,2048]{3,2,1,0:T(8,128)(2,1)}, u32[]{:S(2)}, u32[]{:S(2)}) async-start(bf16[4,16,16,2048]{3,2,1,0:T(8,128)(2,1)} %bitcast.80), calls=%async_computation.3 | async-start | bytes 8388608 | tf_op jit(solution)/shard_map/all_to_all | solution.py:45
  140.3 0.2 reduce-scatter.9.cloned.1.call-start
  140.5 16.4 %convolution_convert_fusion.1 = bf16[128,8192]{1,0:T(8,128)(2,1)} fusion(bf16[2048,8192]{1,0:T(8,128)(2,1)} %param.8, bf16[4,128,2048]{2,1,0:T(8,128)(2,1)S(1)} %copy-done), kind=kOutput, calls=%fused_computation.5 | convolution fusion | flops 4296015872 | bytes 36175872 | tf_op jit(solution)/shard_map/dot_general | solution.py:61
  156.9 17.4 %convolution_convert_fusion = bf16[128,8192]{1,0:T(8,128)(2,1)} fusion(bf16[2048,8192]{1,0:T(8,128)(2,1)} %param.8, bf16[4,128,2048]{2,1,0:T(8,128)(2,1)S(1)} %copy-done), kind=kOutput, calls=%fused_computation.4 | convolution fusion | flops 4296015872 | bytes 36175872 | tf_op jit(solution)/shard_map/dot_general | solution.py:61
  174.4 0.6 copy-done.4
  175.0 0.1 fusion.22
  175.1 4.3 %gather_fusion.1 = bf16[32,16,2048]{2,1,0:T(8,128)(2,1)} fusion(bf16[64,16,2048]{2,1,0:T(8,128)(2,1)} %bitcast.5, s32[1024]{0:T(1024)S(1)} %pad_clamp_fusion), kind=kCustom, calls=%fused_computation.1 | custom fusion | bytes 4194432 | tf_op jit(solution)/shard_map/gather | solution.py:47
  179.4 53.6 %all-to-all-done.2 = bf16[4,16,16,2048]{3,2,1,0:T(8,128)(2,1)} async-done(((bf16[4,16,16,2048]{3,2,1,0:T(8,128)(2,1)}), bf16[4,16,16,2048]{3,2,1,0:T(8,128)(2,1)}, u32[]{:S(2)}, u32[]{:S(2)}) %all-to-all-start.2) | async-done | bytes 4194336 | tf_op jit(solution)/shard_map/all_to_all | solution.py:45
  233.0 4.2 %gather_fusion.3 = bf16[32,16,2048]{2,1,0:T(8,128)(2,1)} fusion(bf16[64,16,2048]{2,1,0:T(8,128)(2,1)} %bitcast.14, s32[1024]{0:T(1024)S(1)} %pad_clamp_fusion), kind=kCustom, calls=%fused_computation.3 | custom fusion | bytes 4194432 | tf_op jit(solution)/shard_map/gather | solution.py:48
  237.2 2.5 fusion
  239.8 13.5 %all-reduce = (f32[8,16,16]{1,2,0:T(8,128)S(1)}, f32[8,16,16]{1,2,0:T(8,128)S(1)}, f32[8,16,16]{1,2,0:T(8,128)S(1)}, f32[8,16,16]{1,2,0:T(8,128)S(1)}) all-reduce(f32[8,16,16]{1,2,0:T(8,128)S(1)} %get-tuple-element.10, f32[8,16,16]{1,2,0:T(8,128)S(1)} %get-tuple-element.11, ...), channel_id=1, replica_groups=mesh['rep'=2,'dp'=4,'tp'=4] {'tp'}, use_global_device_ids=true, to_apply=%region_10.11 | all-reduce | flops 8192 | bytes 65536 | tf_op jit(solution)/shard_map/psum | solution.py:69
  253.3 2.7 fusion.11
  255.9 1.6 fusion.9
  257.5 1.6 fusion.7
  259.1 0.6 fusion.5
  259.8 1.5 fusion.4
  261.4 1.5 fusion.3
  262.9 2.0 fusion.2
  264.9 1.2 fusion.1
  266.2 1.6 pad_maximum_fusion
  (29 shorter events, 0.3 us)
Async XLA Ops:
  9.1 22.9 %all-to-all-start = ((s32[4,1,16]{2,1,0:T(1,128)}), s32[4,1,16]{2,1,0:T(1,128)S(1)}, u32[]{:S(2)}, u32[]{:S(2)}) async-start(s32[4,1,16]{2,1,0:T(1,128)} %bitcast.2), calls=%async_computation.1 | async-start | bytes 4096 | tf_op jit(solution)/shard_map/all_to_all | solution.py:41
  15.4 244.4 %reduce-scatter.5.cloned.1.call-start = ((), (), s32[]{:S(2)}) async-start(), calls=%async_computation.7 | async-start | bytes 2621440 | tf_op jit(solution)/shard_map/reduce_scatter | solution.py:66
  37.1 5.2 %copy-start = (bf16[4,128,2048]{2,1,0:T(8,128)(2,1)S(1)}, bf16[4,128,2048]{2,1,0:T(8,128)(2,1)}, u32[]{:S(2)}) copy-start(bf16[4,128,2048]{2,1,0:T(8,128)(2,1)} %param.7) | copy-start | bytes 6291460
  37.1 98.3 %all-to-all-start.1 = ((bf16[4,16,16,2048]{3,2,1,0:T(8,128)(2,1)}), bf16[4,16,16,2048]{3,2,1,0:T(8,128)(2,1)}, u32[]{:S(2)}, u32[]{:S(2)}) async-start(bf16[4,16,16,2048]{3,2,1,0:T(8,128)(2,1)} %bitcast.81), calls=%async_computation.2 | async-start | bytes 8388608 | tf_op jit(solution)/shard_map/all_to_all | solution.py:44
  42.4 219.0 %reduce-scatter.7.cloned.1.call-start = ((), (), s32[]{:S(2)}) async-start(), calls=%async_computation.8 | async-start | bytes 2621440 | tf_op jit(solution)/shard_map/reduce_scatter | solution.py:66
  135.4 97.6 %all-to-all-start.2 = ((bf16[4,16,16,2048]{3,2,1,0:T(8,128)(2,1)}), bf16[4,16,16,2048]{3,2,1,0:T(8,128)(2,1)}, u32[]{:S(2)}, u32[]{:S(2)}) async-start(bf16[4,16,16,2048]{3,2,1,0:T(8,128)(2,1)} %bitcast.80), calls=%async_computation.3 | async-start | bytes 8388608 | tf_op jit(solution)/shard_map/all_to_all | solution.py:45
  140.3 122.6 %reduce-scatter.9.cloned.1.call-start = ((), (), s32[]{:S(2)}) async-start(), calls=%async_computation.9 | async-start | bytes 2621440 | tf_op jit(solution)/shard_map/reduce_scatter | solution.py:66
  156.9 108.0 %reduce-scatter.11.cloned.1.call-start = ((), (), s32[]{:S(2)}) async-start(), calls=%async_computation.10 | async-start | bytes 2621440 | tf_op jit(solution)/shard_map/reduce_scatter | solution.py:66
  174.4 0.7 copy-start.4
  239.7 16.2 %copy-start.1 = (bf16[32,16,2048]{2,1,0:T(8,128)(2,1)S(1)}, bf16[32,16,2048]{2,1,0:T(8,128)(2,1)}, u32[]{:S(2)}) copy-start(bf16[32,16,2048]{2,1,0:T(8,128)(2,1)} %gather_fusion.3) | copy-start | bytes 6291460
  259.7 3.1 %copy-start.2 = (f32[8,16,2048]{2,1,0:T(8,128)S(1)}, f32[8,16,2048]{2,1,0:T(8,128)}, u32[]{:S(2)}) copy-start(f32[8,16,2048]{2,1,0:T(8,128)} %fusion.7) | copy-start | bytes 3145732
  264.9 1.3 copy-start.3
Sparse Core Ops, SparseCore 0:
  32.2 32.8 reduce-scatter.4
  67.8 31.4 reduce-scatter.6
  157.0 32.7 reduce-scatter.8
  192.3 31.4 reduce-scatter.10
where the time goes:
time: 275 us; the launch traced here: 274 us
  waiting for transfers between devices  125 us (45%)
  matrix products  76.2 us (28%)
  local copies, waits for them, and re-layouts  20 us (7%)
  starting transfers between devices  16.7 us (6%)
  blocking collectives  13.5 us (5%)
  between operations  13.3 us (5%)
  other arithmetic  9.73 us (4%)
    all_to_all x1, waiting for transfers between devices, per_device(): lax.all_to_all(located_shrink, 'dp', split_axis=0, concat_axis=0, tiled=T...  71.2 us
    dot_general x4, matrix products, per_device(): jnp.dot(attention_output[decode_step_index], output_projection_weight, pr...  67.2 us
    all_to_all x1, waiting for transfers between devices, per_device(): lax.all_to_all(located_expand, 'dp', split_axis=0, concat_axis=0, tiled=T...  53.6 us
    psum x1, blocking collectives, per_device(): shrink_now = lax.psum(shrink_part[decode_step_index], 'tp')  13.5 us
    dot_general x4, matrix products, per_device(): jnp.einsum('gsr,grd->gsd', shrink_now, selected_expand[decode_step_index]...  6.48 us
    all_to_all x1, starting transfers between devices, per_device(): lax.all_to_all(requests, 'dp', split_axis=0, concat_axis=0, tiled=True)  6.32 us
    convert_element_type x4, other arithmetic, per_device(): (base + delta.reshape(rows_dev, width_dev)).astype(jnp.bfloat16)  6.25 us
  transfers between devices with their start and end apart: 7, of which 2 were waited for; matrix products, arithmetic and copies ran while one was open for 36% of the time, Pallas kernels for 0%

commit v1 on v0

v1 whole, which is shorter than its diff:
```python
import functools

import jax
import jax.numpy as jnp
from jax import lax
from jax.experimental import pallas as pl
from jax.experimental.pallas import tpu as pltpu
from jax.sharding import PartitionSpec as P

NEAR = 208
OWN = 72
SHARED = 64
ROUND = 64
VMEM = 48 * 2**20


def group_of(shape):
    return lax.broadcasted_iota(jnp.int32, shape, 1) // 16


def row_of(shape):
    return lax.broadcasted_iota(jnp.int32, shape, 0) % 8


def fold(v):
    for shift in (64, 32, 16):
        v = v + pltpu.roll(v, shift, axis=1)
    return v


def score_kernel(sizes, *refs):
    m = len(sizes)
    slots, got, a_ref, out_ref, acc = refs[:m], refs[m:2 * m], refs[2 * m], refs[2 * m + 1], refs[2 * m + 2]
    g = pl.program_id(0)
    per = a_ref.shape[0] // 16

    @pl.when(g == 0)
    def _():
        acc[...] = jnp.zeros_like(acc)

    off = 0
    for i, n in enumerate(sizes):
        s = lax.dot_general(
            got[i][...], a_ref[...], (((1,), (1,)), ((), ())), preferred_element_type=jnp.float32
        )
        s = jnp.where(group_of(s.shape) + g * per == slots[i][...], s, 0.0)
        v = s[:, :128]
        for c in range(128, s.shape[1], 128):
            v = v + s[:, c:c + 128]
        acc[off:off + n, :] += v
        off += n

    @pl.when(g == pl.num_programs(0) - 1)
    def _():
        off = 0
        for n in sizes:
            v = fold(acc[off:off + n, :])
            v = jnp.where(group_of(v.shape) == row_of(v.shape), v, 0.0)
            out_ref[off // 8:(off + n) // 8, :] = jnp.sum(v.reshape(n // 8, 8, 128), axis=1)
            off += n


def scores(slots, got, store):
    sizes = tuple(v.shape[0] for v in got)
    total, width = sum(sizes), store.shape[1]
    blk = 256
    whole = lambda v: pl.BlockSpec(v.shape, lambda g: (0, 0))
    return pl.pallas_call(
        functools.partial(score_kernel, sizes),
        grid=(store.shape[0] // blk,),
        in_specs=[whole(v) for v in slots] + [whole(v) for v in got]
        + [pl.BlockSpec((blk, width), lambda g: (g, 0))],
        out_specs=pl.BlockSpec((total // 8, 128), lambda g: (0, 0)),
        out_shape=jax.ShapeDtypeStruct((total // 8, 128), jnp.float32),
        scratch_shapes=[pltpu.VMEM((total, 128), jnp.float32)],
        compiler_params=pltpu.CompilerParams(vmem_limit_bytes=VMEM),
        cost_estimate=pl.CostEstimate(
            flops=2 * total * width * store.shape[0],
            bytes_accessed=2 * width * (total + store.shape[0]),
            transcendentals=0,
        ),
        name="scores",
    )(*slots, *got, store)


def delta_kernel(sizes, *refs):
    m = len(sizes)
    slots, packed, b_ref, outs, spread = refs[:m], refs[m], refs[m + 1], refs[m + 2:2 * m + 2], refs[2 * m + 2:]

    @pl.when(pl.program_id(0) == 0)
    def _():
        off = 0
        for i, n in enumerate(sizes):
            v = packed[off // 8:(off + n) // 8, :]
            v = jnp.broadcast_to(v[:, None, :], (n // 8, 8, 128)).reshape(n, 128)
            group = group_of(v.shape)
            v = fold(jnp.where(group == row_of(v.shape), v, 0.0))
            for c in range(b_ref.shape[0] // 128):
                hit = group + c * 8 == slots[i][...]
                spread[i][:, c * 128:(c + 1) * 128] = jnp.where(hit, v, 0.0).astype(jnp.bfloat16)
            off += n

    for i in range(m):
        outs[i][...] = jnp.dot(
            spread[i][...], b_ref[...], preferred_element_type=jnp.float32
        ).astype(jnp.bfloat16)


def deltas(slots, packed, store):
    sizes = tuple(v.shape[0] for v in slots)
    depth, width = store.shape
    cols = width // 4
    whole = lambda v: pl.BlockSpec(v.shape, lambda g: (0, 0))
    return pl.pallas_call(
        functools.partial(delta_kernel, sizes),
        grid=(width // cols,),
        in_specs=[whole(v) for v in slots] + [whole(packed)]
        + [pl.BlockSpec((depth, cols), lambda g: (0, g))],
        out_specs=[pl.BlockSpec((n, cols), lambda g: (0, g)) for n in sizes],
        out_shape=[jax.ShapeDtypeStruct((n, width), jnp.bfloat16) for n in sizes],
        scratch_shapes=[pltpu.VMEM((n, depth), jnp.bfloat16) for n in sizes],
        compiler_params=pltpu.CompilerParams(vmem_limit_bytes=VMEM),
        cost_estimate=pl.CostEstimate(
            flops=2 * sum(sizes) * width * depth,
            bytes_accessed=2 * width * (sum(sizes) + depth),
            transcendentals=0,
        ),
        name="deltas",
    )(*slots, packed, store)


def finish_kernel(m, a, row_ref, *refs):
    codes, back, adds, out_ref = refs[:m], refs[m:2 * m], refs[2 * m:2 * m + a], refs[2 * m + a]
    total = adds[0][...].astype(jnp.float32)
    for v in adds[1:]:
        total += v[...].astype(jnp.float32)
    for code, b in zip(codes, back):
        put = jnp.where(row_ref[...] == code[...], 1.0, 0.0).astype(jnp.bfloat16)
        total += jnp.dot(put, b[...], preferred_element_type=jnp.float32)
    out_ref[...] = total.astype(out_ref.dtype)


def finish(row_code, codes, back, adds):
    rows, width = adds[0].shape
    cols = width // 4
    whole = lambda v: pl.BlockSpec(v.shape, lambda g: (0, 0))
    part = lambda v: pl.BlockSpec((v.shape[0], cols), lambda g: (0, g))
    return pl.pallas_call(
        functools.partial(finish_kernel, len(codes), len(adds)),
        grid=(width // cols,),
        in_specs=[whole(row_code)] + [whole(v) for v in codes] + [part(v) for v in back] + [part(v) for v in adds],
        out_specs=pl.BlockSpec((rows, cols), lambda g: (0, g)),
        out_shape=jax.ShapeDtypeStruct((rows, width), jnp.bfloat16),
        compiler_params=pltpu.CompilerParams(vmem_limit_bytes=VMEM),
        name="finish",
    )(row_code, *codes, *back, *adds)


def per_device(
    attention_output,
    output_projection_weight,
    shrink_matrix_store,
    expand_matrix_store,
    segment_adapter,
    segment_live_rows,
    adapter_store_index,
):
    steps, rows_dev, width = attention_output.shape
    seg_count = segment_adapter.shape[1]
    seg_len = rows_dev // seg_count
    store, rank, _ = shrink_matrix_store.shape
    n_rep, n_dp, n_tp = (lax.axis_size(a) for a in ("rep", "dp", "tp"))
    me = lax.axis_index("dp")
    rows = steps * rows_dev
    count = steps * seg_count
    big = 2 * rows

    x = attention_output.reshape(rows, width)
    shrink_store = shrink_matrix_store.reshape(store * rank, width)
    expand_store = expand_matrix_store.reshape(store * rank, width)
    far = range(2, n_dp)

    def swap(v, axis, k):
        n = lax.axis_size(axis)
        return lax.ppermute(v, axis, [(i, i ^ k) for i in range(n)])

    def butterfly(v, axis, op):
        k = 1
        while k < lax.axis_size(axis):
            v = op(v, swap(v, axis, k))
            k *= 2
        return v

    ids = segment_adapter.reshape(count)
    lives = segment_live_rows.reshape(count)
    index = jnp.arange(adapter_store_index.shape[0], dtype=jnp.int32)
    position = jnp.sum(
        jnp.where(ids[:, None] == index[None, :], adapter_store_index[None, :], 0), axis=1
    )
    table = jnp.stack([position, lives])
    tables = [table] + [swap(table, "dp", k) for k in range(1, n_dp)]

    order = jnp.arange(count, dtype=jnp.int32)

    def layout(k):
        pos, alive = tables[k][0], tables[k][1]
        dist = (pos // store) ^ (me ^ k)
        before = (dist[:, None] == dist[None, :]) & (order[:, None] > order[None, :])
        start = jnp.sum(jnp.where(before, alive[None, :], 0), axis=1)
        totals = [jnp.sum(jnp.where(dist == j, alive, 0)) for j in range(n_dp)]
        held, over = [None, jnp.int32(NEAR)], [None, None]
        for j in range(2, n_dp, 2):
            extra = jnp.maximum(totals[j] - OWN, 0)
            over += [extra, extra]
            held += [jnp.int32(OWN + 2 * SHARED), OWN + jnp.maximum(2 * SHARED - extra, 0)]
        left = functools.reduce(jnp.maximum, [totals[j] - held[j] for j in range(1, n_dp)])
        return dict(dist=dist, slot=pos % store, alive=alive, start=start, held=held, over=over, left=left)

    lay = [layout(k) for k in range(n_dp)]

    def near():
        return big + jnp.arange(NEAR, dtype=jnp.int32)

    def own(j):
        return j * big + jnp.arange(OWN, dtype=jnp.int32)

    def shared(k, j):
        f = jnp.arange(SHARED, dtype=jnp.int32) + (j % 2) * SHARED
        even, over = j - j % 2, lay[k]["over"][j]
        return OWN + jnp.where(f < over, even * big + f, (even + 1) * big + f - over)

    def late(k, j, low):
        return j * big + lay[k]["held"][j] + low + jnp.arange(ROUND, dtype=jnp.int32)

    def slots_of(k, code):
        seg = lay[k]["dist"] * big + lay[k]["start"]
        hit = (code[:, None] >= seg[None, :]) & (code[:, None] < (seg + lay[k]["alive"])[None, :])
        hit = hit & (lay[k]["dist"] == k)[None, :]
        return jnp.max(jnp.where(hit, lay[k]["slot"][None, :], -1), axis=1, keepdims=True)

    lane = jnp.arange(seg_len, dtype=jnp.int32)
    live = lane[None, :] < lives[:, None]
    row_code = (lay[0]["dist"] * big + lay[0]["start"])[:, None] + lane[None, :]
    row_code = jnp.where(live, row_code, -1).reshape(rows)
    self_slots = jnp.where(live & (lay[0]["dist"] == 0)[:, None], lay[0]["slot"][:, None], -1).reshape(rows, 1)

    def pack(code):
        pick = (code[:, None] == row_code[None, :]).astype(jnp.bfloat16)
        return jnp.dot(pick, x, preferred_element_type=jnp.float32).astype(jnp.bfloat16)

    def answer(slots, got):
        part = butterfly(scores(slots, got, shrink_store), "tp", jnp.add)
        return deltas(slots, part, expand_store)

    out_shared = {j: pack(shared(0, j)) for j in far}
    out_own = {j: pack(own(j)) for j in far}
    out_near = pack(near())
    weight, out_shared, out_own, out_near = lax.optimization_barrier(
        (output_projection_weight, out_shared, out_own, out_near)
    )
    in_shared = {j: swap(out_shared[j], "dp", j) for j in far}
    in_own = {j: swap(out_own[j], "dp", j) for j in far}
    in_near = swap(out_near, "dp", 1)
    in_relay = {j: swap(in_shared[j], "dp", 1) for j in far}

    at = lax.axis_index("tp")
    cols = weight.shape[1] // n_tp

    def share(k):
        w = lax.dynamic_slice_in_dim(weight, (at ^ k) * cols, cols, axis=1)
        return jnp.dot(x, w, preferred_element_type=jnp.float32).astype(jnp.bfloat16)

    held = {k: [share(k)] for k in reversed(range(n_tp))}
    bit = 1
    while bit < n_tp:
        for k in sorted((k for k in held if k & bit), reverse=True):
            v = held.pop(k)
            if len(v) > 1:
                v = [functools.reduce(jnp.add, [u.astype(jnp.float32) for u in v]).astype(jnp.bfloat16)]
            held[k ^ bit].append(swap(v[0], "tp", bit))
        bit *= 2
    base = held[0]

    (self_delta,) = answer([self_slots], [x])

    slots_s = [slots_of(j, shared(j, j)) for j in far]
    slots_r = [slots_of(j ^ 1, shared(j ^ 1, j)) for j in far]
    both = answer(slots_s + slots_r, [in_shared[j] for j in far] + [in_relay[j] for j in far])
    back_shared = []
    for i, j in enumerate(far):
        v = both[i] + swap(both[len(far) + i], "dp", 1)
        back_shared.append(swap(v, "dp", j))

    slots_o = [slots_of(j, own(j)) for j in far] + [slots_of(1, near())]
    direct = answer(slots_o, [in_own[j] for j in far] + [in_near])
    back_own = [swap(direct[i], "dp", j) for i, j in enumerate(far)]
    back_near = swap(direct[-1], "dp", 1)

    codes = [shared(0, j) for j in far] + [own(j) for j in far] + [near()]
    codes = [v.reshape(1, -1) for v in codes]
    back = back_shared + back_own + [back_near]
    adds = base + [self_delta]

    left = functools.reduce(jnp.maximum, [v["left"] for v in lay])
    left = butterfly(left.reshape(1), "rep", jnp.maximum)[0]

    def rest(args):
        row_code, codes, back, adds = args

        def body(i, extra):
            low = i * ROUND
            got = [swap(pack(late(0, j, low)), "dp", j) for j in range(1, n_dp)]
            slots = [slots_of(j, late(j, j, low)) for j in range(1, n_dp)]
            for j, v in zip(range(1, n_dp), answer(slots, got)):
                put = (row_code == late(0, j, low)[None, :]).astype(jnp.bfloat16)
                extra = extra + jnp.dot(put, swap(v, "dp", j), preferred_element_type=jnp.float32)
            return extra

        rounds = (left + ROUND - 1) // ROUND
        extra = lax.fori_loop(0, rounds, body, jnp.zeros((rows, width), jnp.float32))
        return finish(row_code, codes, back, adds + [extra])

    out = lax.cond(left > 0, rest, lambda args: finish(*args), (row_code.reshape(rows, 1), codes, back, adds))
    return out.reshape(steps, rows_dev, width)


def solution(mesh):
    return jax.shard_map(
        per_device,
        mesh=mesh,
        in_specs=(
            P(None, ("rep", "dp"), "tp"),
            P("tp", None),
            P("dp", None, "tp"),
            P("dp", None, "tp"),
            P(None, ("rep", "dp")),
            P(None, ("rep", "dp")),
            P("rep"),
        ),
        out_specs=P(None, ("rep", "dp"), "tp"),
        check_vma=False,
    )
```

time: 275 us -> 216 us (0.79)
  waiting for transfers between devices: 125 us -> 29.1 us
  Pallas kernels: 0 us -> 39.8 us
  starting transfers between devices: 16.7 us -> 48.5 us
  matrix products: 76.2 us -> 46.5 us
  blocking collectives: 13.5 us -> 0 us
  other arithmetic: 9.73 us -> 17.5 us
    all_to_all x3 -> x0, waiting for transfers between devices: 125 us -> none  [the longest x1 71.2 us: per_device(): lax.all_to_all(located_shrink, 'dp', split_axis=0, concat_axis=0, tiled=T...]
    ppermute x0 -> x27, starting transfers between devices: none -> 48.5 us  [swap(): return lax.ppermute(v, axis, [(i, i ^ k) for i in range(n)])]
    pallas_call x0 -> x7, Pallas kernels: none -> 39.8 us  [the longest x3 18.5 us: scores(): pl.pallas_call(functools.partial(score_kernel, sizes), grid=(store.shape[...]
    dot_general x9, matrix products: 76.2 us -> 46.5 us  [the longest x4 39.1 us: share(): jnp.dot(x, w, preferred_element_type=jnp.float32).astype(jnp.bfloat16)]
    ppermute x0 -> x27, waiting for transfers between devices: none -> 29.1 us  [swap(): return lax.ppermute(v, axis, [(i, i ^ k) for i in range(n)])]
    gather x4 -> x0, local copies, waits for them, and re-layouts: 18.4 us -> none  [the longest x1 4.98 us: per_device(): located_expand = expand_matrix_store[requested_adapter]]
    all_to_all x3 -> x0, starting transfers between devices: 16.4 us -> none  [the longest x1 6.32 us: per_device(): lax.all_to_all(requests, 'dp', split_axis=0, concat_axis=0, tiled=True)]
    psum x1 -> x0, blocking collectives: 13.5 us -> none  [per_device(): shrink_now = lax.psum(shrink_part[decode_step_index], 'tp')]
  transfers between devices with their start and end apart: 7 -> 27, of which waited for: 2 -> 8; matrix products, arithmetic and copies ran while one was open for 36% -> 31% of each run, Pallas kernels for 0% -> 16%
where the time goes in v1:
time: 216 us; the launch traced here: 215 us
  starting transfers between devices  48.5 us (22%)
  matrix products  46.5 us (22%)
  Pallas kernels  39.8 us (18%)
  waiting for transfers between devices  29.1 us (13%)
  local copies, waits for them, and re-layouts  22.4 us (10%)
  other arithmetic  17.5 us (8%)
  between operations  11 us (5%)
    ppermute x27, starting transfers between devices, swap(): return lax.ppermute(v, axis, [(i, i ^ k) for i in range(n)])  48.5 us
    dot_general x4, matrix products, share(): jnp.dot(x, w, preferred_element_type=jnp.float32).astype(jnp.bfloat16)  39.1 us
    ppermute x27, waiting for transfers between devices, swap(): return lax.ppermute(v, axis, [(i, i ^ k) for i in range(n)])  29.1 us
    pallas_call x3, Pallas kernels, scores(): pl.pallas_call(functools.partial(score_kernel, sizes), grid=(store.shape[...  18.5 us
    pallas_call x3, Pallas kernels, deltas(): pl.pallas_call(functools.partial(delta_kernel, sizes), grid=(width // col...  15.4 us
    another operation x4, local copies, waits for them, and re-layouts  11 us
    dot_general x5, matrix products, pack(): jnp.dot(pick, x, preferred_element_type=jnp.float32).astype(jnp.bfloat16)  7.33 us
    reduce_sum x4, other arithmetic, layout(): totals = [jnp.sum(jnp.where(dist == j, alive, 0)) for j in range(n_dp)]  7.31 us
  transfers between devices with their start and end apart: 27, of which 8 were waited for; matrix products, arithmetic and copies ran while one was open for 31% of the time, Pallas kernels for 16%

profile of v1, /device:TPU:0, one launch (start us, length us, event | category | flops | bytes accessed | tf_op | source)
XLA Modules:
  0.0 215.1 jit_solution(7154622882655909367)
XLA Ops:
  3.1 4.0 %collective-permute-start.9 = (s32[2,32]{1,0:T(2,128)}, s32[2,32]{1,0:T(2,128)}, u32[]{:S(2)}, u32[]{:S(2)}) collective-permute-start(s32[2,32]{1,0:T(2,128)} %pad_add_fusion), channel_id=1, source_target_pairs={{0,8},{4,12},{8,0},{12,4},{1,9},{5,13},{9,1},{13,5},{2,10},{6,14},... | collective-permute-start | bytes 776 | tf_op jit(solution)/shard_map/ppermute | solution.py:185
  12.2 2.8 %convolution_convert_fusion.6 = bf16[64,2048]{1,0:T(8,128)(2,1)} fusion(bf16[512,2048]{1,0:T(8,128)(2,1)} %bitcast.188, s32[512]{0:T(512)S(1)} %select_n.350, s32[64]{0:T(128)S(1)} %get-tuple-element.813), kind=kOutput, calls=%fused_computation.62 | convolution fusion | flops 134381568 | bytes 2361600 | tf_op jit(solution)/shard_map/dot_general | solution.py:249
  19.5 9.4 %fusion.44 = bf16[512,2048]{0,1:T(8,128)(2,1)} fusion(bf16[512,2048]{1,0:T(8,128)(2,1)S(1)} %bitcast.195, bf16[2048,8192]{1,0:T(8,128)(2,1)} %param.12, s32[]{:T(128)S(6)} %select_n.361), kind=kOutput, calls=%fused_computation.56 | convolution fusion | flops 4296015872 | bytes 12582916 | tf_op jit(solution)/shard_map/dot_general | solution.py:271
  30.9 5.1 %scores.8 = f32[64,128]{1,0:T(8,128)S(1)} custom-call(s32[512,1]{1,0:T(8,128)S(1)} %select_n.365.refs_0_, bf16[512,2048]{1,0:T(8,128)(2,1)S(1)} %bitcast.196, bf16[1024,2048]{1,0:T(8,128)(2,1)} %bitcast.199), custom_call_target="tpu_custom_call" | custom-call | flops 2147483648 | bytes 6291456 | tf_op jit(solution)/shard_map/scores/pallas_call | solution.py:68
  40.6 2.0 fusion.88
  43.9 2.0 fusion.91
  47.2 2.5 %collective-permute-start.13 = (bf16[64,2048]{1,0:T(8,128)(2,1)}, bf16[64,2048]{1,0:T(8,128)(2,1)S(1)}, u32[]{:S(2)}, u32[]{:S(2)}) collective-permute-start(bf16[64,2048]{1,0:T(8,128)(2,1)} %convolution_convert_fusion.6), channel_id=1, source_target_pairs={{0,12},{4,8},{8,4},{12,0},{1,13},{5,9},{9,5},{13,1},{2,14},{6,10},... | collective-permute-start | bytes 786440 | tf_op jit(solution)/shard_map/ppermute | solution.py:185
  57.1 5.2 %collective-permute-done.12.refs_4_ = bf16[64,2048]{1,0:T(8,128)(2,1)S(1)} collective-permute-done((bf16[64,2048]{1,0:T(8,128)(2,1)}, bf16[64,2048]{1,0:T(8,128)(2,1)S(1)}, u32[]{:S(2)}, u32[]{:S(2)}) %collective-permute-start.12) | collective-permute-done | bytes 262176 | tf_op jit(solution)/shard_map/ppermute | solution.py:185
  62.3 7.7 %collective-permute-start.14 = (bf16[64,2048]{1,0:T(8,128)(2,1)S(1)}, bf16[64,2048]{1,0:T(8,128)(2,1)S(1)}, u32[]{:S(2)}, u32[]{:S(2)}) collective-permute-start(bf16[64,2048]{1,0:T(8,128)(2,1)S(1)} %collective-permute-done.12.refs_4_), channel_id=1, source_target_pairs={{0,4},{4,0},{8,12},{12,8},{1,5},{5,1},{9,13},{13,9},{2,6},{6,2},{1... | collective-permute-start | bytes 786440 | tf_op jit(solution)/shard_map/ppermute | solution.py:185
  70.8 5.0 %collective-permute-start.15 = (bf16[64,2048]{1,0:T(8,128)(2,1)S(1)}, bf16[64,2048]{1,0:T(8,128)(2,1)S(1)}, u32[]{:S(2)}, u32[]{:S(2)}) collective-permute-start(bf16[64,2048]{1,0:T(8,128)(2,1)S(1)} %collective-permute-done.13.refs_5_), channel_id=1, source_target_pairs={{0,4},{4,0},{8,12},{12,8},{1,5},{5,1},{9,13},{13,9},{2,6},{6,2},{1... | collective-permute-start | bytes 786440 | tf_op jit(solution)/shard_map/ppermute | solution.py:185
  76.5 3.3 %collective-permute-start.23 = (bf16[72,2048]{1,0:T(8,128)(2,1)S(1)}, bf16[72,2048]{1,0:T(8,128)(2,1)S(1)}, u32[]{:S(2)}, u32[]{:S(2)}) collective-permute-start(bf16[72,2048]{1,0:T(8,128)(2,1)S(1)} %convolution_convert_fusion.4), channel_id=1, source_target_pairs={{0,12},{4,8},{8,4},{12,0},{1,13},{5,9},{9,5},{13,1},{2,14},{6,10},... | collective-permute-start | bytes 884744 | tf_op jit(solution)/shard_map/ppermute | solution.py:185
  79.8 2.8 %collective-permute-done.15.refs_7_ = bf16[64,2048]{1,0:T(8,128)(2,1)S(1)} collective-permute-done((bf16[64,2048]{1,0:T(8,128)(2,1)S(1)}, bf16[64,2048]{1,0:T(8,128)(2,1)S(1)}, u32[]{:S(2)}, u32[]{:S(2)}) %collective-permute-start.15) | collective-permute-done | bytes 262176 | tf_op jit(solution)/shard_map/ppermute | solution.py:185
  82.6 7.1 %scores.6 = f32[32,128]{1,0:T(8,128)S(1)} custom-call(s32[64,1]{1,0:T(8,128)S(1)} %copy.79.refs_0_, s32[64,1]{1,0:T(8,128)S(1)} %copy.80.refs_1_, s32[64,1]{1,0:T(8,128)S(1)} %copy.81.refs_2_, s32[64,1]{1,0:T(8,128)S(1)} %copy.82.refs_3_, bf16[64,2048]{1,0:T(8,128)(2,1)S(1)} %collective-permute-done.12.refs_4_, ...), custom_call_target="tpu_custom_call" | custom-call | flops 1073741824 | bytes 5242880 | tf_op jit(solution)/shard_map/scores/pallas_call | solution.py:68
  94.7 6.3 %scores.7 = f32[44,128]{1,0:T(8,128)S(1)} custom-call(s32[72,1]{1,0:T(8,128)S(1)} %copy.86.refs_0_, s32[72,1]{1,0:T(8,128)S(1)} %copy.87.refs_1_, s32[208,1]{1,0:T(8,128)S(1)} %copy.88.refs_2_, bf16[72,2048]{1,0:T(8,128)(2,1)S(1)} %collective-permute-done.22.refs_3_, bf16[72,2048]{1,0:T(8,128)(2,1)S(1)} %collective-permute-done.23.refs_4_, ...), custom_call_target="tpu_custom_call" | custom-call | flops 1476395008 | bytes 5636096 | tf_op jit(solution)/shard_map/scores/pallas_call | solution.py:68
  101.5 4.6 %deltas.6 = (bf16[64,2048]{1,0:T(8,128)(2,1)S(1)}, bf16[64,2048]{1,0:T(8,128)(2,1)S(1)}, bf16[64,2048]{1,0:T(8,128)(2,1)S(1)}, bf16[64,2048]{1,0:T(8,128)(2,1)S(1)}) custom-call(s32[64,1]{1,0:T(8,128)S(1)} %copy.79.refs_0_, s32[64,1]{1,0:T(8,128)S(1)} %copy.80.refs_1_, s32[64,1]{1,0:T(8,128)S(1)} %copy.81.refs_2_, s32[64,1]{1,0:T(8,128)S(1)} %copy.82.refs_3_, ...), custom_call_target="tpu_custom_call" | custom-call | flops 1073741824 | bytes 5242880 | tf_op jit(solution)/shard_map/deltas/pallas_call | solution.py:114
  106.1 2.5 %collective-permute-start.20 = (bf16[64,2048]{1,0:T(8,128)(2,1)S(1)}, bf16[64,2048]{1,0:T(8,128)(2,1)S(1)}, u32[]{:S(2)}, u32[]{:S(2)}) collective-permute-start(bf16[64,2048]{1,0:T(8,128)(2,1)S(1)} %get-tuple-element.478), channel_id=1, source_target_pairs={{0,4},{4,0},{8,12},{12,8},{1,5},{5,1},{9,13},{13,9},{2,6},{6,2},{1... | collective-permute-start | bytes 786440 | tf_op jit(solution)/shard_map/ppermute | solution.py:185
  110.4 9.5 %fusion.47 = bf16[512,2048]{0,1:T(8,128)(2,1)} fusion(bf16[512,2048]{1,0:T(8,128)(2,1)S(1)} %bitcast.197, bf16[2048,8192]{1,0:T(8,128)(2,1)} %param.12, s32[]{:T(128)S(6)} %select_n.359), kind=kOutput, calls=%fused_computation.57 | convolution fusion | flops 4296015872 | bytes 12582916 | tf_op jit(solution)/shard_map/dot_general | solution.py:271
  128.0 2.9 %collective-permute-start.11 = (s32[1]{0:T(128)}, s32[1]{0:T(128)}, u32[]{:S(2)}, u32[]{:S(2)}) collective-permute-start(s32[1]{0:T(128)} %bitcast.13), channel_id=1, source_target_pairs={{0,16},{16,0},{1,17},{17,1},{2,18},{18,2},{3,19},{19,3},{4,20},{20... | collective-permute-start | bytes 20 | tf_op jit(solution)/shard_map/ppermute | solution.py:185
  132.3 3.0 %collective-permute-start.21 = (bf16[64,2048]{1,0:T(8,128)(2,1)S(1)}, bf16[64,2048]{1,0:T(8,128)(2,1)S(1)}, u32[]{:S(2)}, u32[]{:S(2)}) collective-permute-start(bf16[64,2048]{1,0:T(8,128)(2,1)S(1)} %add.760), channel_id=1, source_target_pairs={{0,12},{4,8},{8,4},{12,0},{1,13},{5,9},{9,5},{13,1},{2,14},{6,10},... | collective-permute-start | bytes 786440 | tf_op jit(solution)/shard_map/ppermute | solution.py:185
  135.3 10.8 %fusion.31 = bf16[512,2048]{0,1:T(8,128)(2,1)} fusion(bf16[512,2048]{0,1:T(8,128)(2,1)} %collective-permute-done.31, bf16[512,2048]{1,0:T(8,128)(2,1)} %bitcast.189, bf16[2048,8192]{1,0:T(8,128)(2,1)} %param.12, s32[]{:T(128)S(6)} %select_n.360), kind=kOutput, calls=%fused_computation.51 | convolution fusion | flops 4300210176 | bytes 14680068 | tf_op jit(solution)/shard_map/dot_general | solution.py:271
  147.6 4.3 %deltas.7 = (bf16[72,2048]{1,0:T(8,128)(2,1)S(1)}, bf16[72,2048]{1,0:T(8,128)(2,1)S(1)}, bf16[208,2048]{1,0:T(8,128)(2,1)S(1)}) custom-call(s32[72,1]{1,0:T(8,128)S(1)} %copy.86.refs_0_, s32[72,1]{1,0:T(8,128)S(1)} %copy.87.refs_1_, s32[208,1]{1,0:T(8,128)S(1)} %copy.88.refs_2_, f32[44,128]{1,0:T(8,128)S(1)} %add.765.refs_3_, bf16[1024,2048]{1,0:T(8,128)(2,1)S(1)} %bitcast.206), custom_call_target="tpu_custom_call" | custom-call | flops 1476395008 | bytes 5636096 | tf_op jit(solution)/shard_map/deltas/pallas_call | solution.py:114
  153.3 9.5 %fusion.50 = bf16[512,2048]{0,1:T(8,128)(2,1)} fusion(bf16[512,2048]{1,0:T(8,128)(2,1)S(1)} %bitcast.198, bf16[2048,8192]{1,0:T(8,128)(2,1)} %param.12, s32[]{:T(128)S(6)} %select_n.358), kind=kOutput, calls=%fused_computation.58 | convolution fusion | flops 4296015872 | bytes 12582916 | tf_op jit(solution)/shard_map/dot_general | solution.py:271
  164.0 2.1 collective-permute-start.27
  169.0 6.6 %deltas.8 = bf16[512,2048]{1,0:T(8,128)(2,1)} custom-call(s32[512,1]{1,0:T(8,128)S(1)} %select_n.365.refs_0_, f32[64,128]{1,0:T(8,128)S(1)} %add.773.refs_1_, bf16[1024,2048]{1,0:T(8,128)(2,1)} %bitcast.203), custom_call_target="tpu_custom_call" | custom-call | flops 2147483648 | bytes 6291456 | tf_op jit(solution)/shard_map/deltas/pallas_call | solution.py:114
  175.5 8.4 %collective-permute-done.27 = bf16[72,2048]{1,0:T(8,128)(2,1)S(1)} collective-permute-done((bf16[72,2048]{1,0:T(8,128)(2,1)S(1)}, bf16[72,2048]{1,0:T(8,128)(2,1)S(1)}, u32[]{:S(2)}, u32[]{:S(2)}) %collective-permute-start.27) | collective-permute-done | bytes 294944 | tf_op jit(solution)/shard_map/ppermute | solution.py:185
  183.9 7.1 %collective-permute-done.28 = bf16[72,2048]{1,0:T(8,128)(2,1)S(1)} collective-permute-done((bf16[72,2048]{1,0:T(8,128)(2,1)S(1)}, bf16[72,2048]{1,0:T(8,128)(2,1)S(1)}, u32[]{:S(2)}, u32[]{:S(2)}) %collective-permute-start.28) | collective-permute-done | bytes 294944 | tf_op jit(solution)/shard_map/ppermute | solution.py:185
  191.0 2.0 collective-permute-done.32
  194.2 19.5 %conditional.1 = (bf16[4,128,2048]{2,1,0:T(8,128)(2,1)S(1)}) conditional(s32[]{:T(128)} %convert_element_type.78, (s32[512,1]{0,1:T(1,128)S(1)}, s32[1,64]{1,0:T(1,128)}, s32[1,64]{1,0:T(1,128)}, s32[1,72]{1,0:T(1,128)}, s32[1,72]{1,0:T(1,128)}, /*index=5*/s32[1,208]{1,0:T(1,128)}, bf16[64,2048]{1,0:T(8,128)(2,1)}, bf16[64,2048]{1,0:T(8,128)(2,1)}, ...), branch_computations={%region_24.25_spmd, %region_25.31_spmd} | conditional | flops 2419700224 | bytes 143759040 | solution.py:323
  195.0 2.9 %copy.92.refs_10_ = bf16[512,2048]{1,0:T(8,128)(2,1)S(1)} copy(bf16[512,2048]{0,1:T(8,128)(2,1)} %get-tuple-element.670) | data formatting | bytes 4194304 | tf_op jit(solution)/shard_map
  197.9 4.0 %copy.93.refs_11_ = bf16[512,2048]{1,0:T(8,128)(2,1)} copy(bf16[512,2048]{0,1:T(8,128)(2,1)} %get-tuple-element.671) | data formatting | bytes 4194304 | tf_op jit(solution)/shard_map
  201.9 4.0 %copy.94.refs_12_ = bf16[512,2048]{1,0:T(8,128)(2,1)} copy(bf16[512,2048]{0,1:T(8,128)(2,1)} %get-tuple-element.672) | data formatting | bytes 4194304 | tf_op jit(solution)/shard_map
  207.6 5.9 %finish.2 = bf16[512,2048]{1,0:T(8,128)(2,1)S(1)} custom-call(s32[512,1]{1,0:T(8,128)S(1)} %copy.91.row_ref, s32[1,64]{1,0:T(1,128)S(1)} %copy-done.45, s32[1,64]{1,0:T(1,128)S(1)} %copy-done.47, s32[1,72]{1,0:T(1,128)S(1)} %copy-done.51, s32[1,72]{1,0:T(1,128)S(1)} %copy-done.49, s32[1,208]{1,0:T(1,128)S(1)} %copy-done.42, ...), custom_call_target="tpu_custom_call" | custom-call | tf_op jit(solution)/shard_map/cond/branch_0_fun/finish/pallas_call | solution.py:148
  (176 shorter events, 48.8 us)
Async XLA Ops:
  3.1 33.0 %collective-permute-start.9 = (s32[2,32]{1,0:T(2,128)}, s32[2,32]{1,0:T(2,128)}, u32[]{:S(2)}, u32[]{:S(2)}) collective-permute-start(s32[2,32]{1,0:T(2,128)} %pad_add_fusion), channel_id=1, source_target_pairs={{0,8},{4,12},{8,0},{12,4},{1,9},{5,13},{9,1},{13,5},{2,10},{6,14},... | collective-permute-start | bytes 776 | tf_op jit(solution)/shard_map/ppermute | solution.py:185
  7.2 31.4 %collective-permute-start.10 = (s32[2,32]{1,0:T(2,128)}, s32[2,32]{1,0:T(2,128)}, u32[]{:S(2)}, u32[]{:S(2)}) collective-permute-start(s32[2,32]{1,0:T(2,128)} %pad_add_fusion), channel_id=1, source_target_pairs={{0,12},{4,8},{8,4},{12,0},{1,13},{5,9},{9,5},{13,1},{2,14},{6,10},... | collective-permute-start | bytes 776 | tf_op jit(solution)/shard_map/ppermute | solution.py:185
  8.5 38.6 %collective-permute-start.8 = (s32[2,32]{1,0:T(2,128)}, s32[2,32]{1,0:T(2,128)}, u32[]{:S(2)}, u32[]{:S(2)}) collective-permute-start(s32[2,32]{1,0:T(2,128)} %pad_add_fusion), channel_id=1, source_target_pairs={{0,4},{4,0},{8,12},{12,8},{1,5},{5,1},{9,13},{13,9},{2,6},{6,2},{1... | collective-permute-start | bytes 776 | tf_op jit(solution)/shard_map/ppermute | solution.py:185
  29.0 106.3 %collective-permute-start.31 = (bf16[512,2048]{0,1:T(8,128)(2,1)}, bf16[512,2048]{0,1:T(8,128)(2,1)}, u32[]{:S(2)}, u32[]{:S(2)}) collective-permute-start(bf16[512,2048]{0,1:T(8,128)(2,1)} %fusion.44), channel_id=1, source_target_pairs={{0,1},{1,0},{2,3},{3,2},{4,5},{5,4},{6,7},{7,6},{8,9},{9,8},{10,11... | collective-permute-start | bytes 6291464 | tf_op jit(solution)/shard_map/ppermute | solution.py:185
  29.0 65.7 %collective-permute-start.24 = (bf16[208,2048]{1,0:T(8,128)(2,1)}, bf16[208,2048]{1,0:T(8,128)(2,1)S(1)}, u32[]{:S(2)}, u32[]{:S(2)}) collective-permute-start(bf16[208,2048]{1,0:T(8,128)(2,1)} %convolution_convert_fusion.3), channel_id=1, source_target_pairs={{0,4},{4,0},{8,12},{12,8},{1,5},{5,1},{9,13},{13,9},{2,6},{6,2},{1... | collective-permute-start | bytes 2555912 | tf_op jit(solution)/shard_map/ppermute | solution.py:185
  36.1 58.6 %collective-permute-start.22 = (bf16[72,2048]{1,0:T(8,128)(2,1)}, bf16[72,2048]{1,0:T(8,128)(2,1)S(1)}, u32[]{:S(2)}, u32[]{:S(2)}) collective-permute-start(bf16[72,2048]{1,0:T(8,128)(2,1)} %convolution_convert_fusion.5), channel_id=1, source_target_pairs={{0,8},{4,12},{8,0},{12,4},{1,9},{5,13},{9,1},{13,5},{2,10},{6,14},... | collective-permute-start | bytes 884744 | tf_op jit(solution)/shard_map/ppermute | solution.py:185
  38.6 23.8 %collective-permute-start.12 = (bf16[64,2048]{1,0:T(8,128)(2,1)}, bf16[64,2048]{1,0:T(8,128)(2,1)S(1)}, u32[]{:S(2)}, u32[]{:S(2)}) collective-permute-start(bf16[64,2048]{1,0:T(8,128)(2,1)} %convolution_convert_fusion.7), channel_id=1, source_target_pairs={{0,8},{4,12},{8,0},{12,4},{1,9},{5,13},{9,1},{13,5},{2,10},{6,14},... | collective-permute-start | bytes 786440 | tf_op jit(solution)/shard_map/ppermute | solution.py:185
  43.9 32.1 %copy-start.20 = (s32[32]{0:T(128)}, s32[32]{0:T(128)S(1)}, u32[]{:S(2)}) copy-start(s32[32]{0:T(128)S(1)} %select_reduce_fusion.13) | copy-start | bytes 388
  47.1 28.9 %copy-start.22 = (s32[32]{0:T(128)}, s32[32]{0:T(128)S(1)}, u32[]{:S(2)}) copy-start(s32[32]{0:T(128)S(1)} %select_reduce_fusion.11) | copy-start | bytes 388
  47.2 23.7 %collective-permute-start.13 = (bf16[64,2048]{1,0:T(8,128)(2,1)}, bf16[64,2048]{1,0:T(8,128)(2,1)S(1)}, u32[]{:S(2)}, u32[]{:S(2)}) collective-permute-start(bf16[64,2048]{1,0:T(8,128)(2,1)} %convolution_convert_fusion.6), channel_id=1, source_target_pairs={{0,12},{4,8},{8,4},{12,0},{1,13},{5,9},{9,5},{13,1},{2,14},{6,10},... | collective-permute-start | bytes 786440 | tf_op jit(solution)/shard_map/ppermute | solution.py:185
  51.5 24.5 %copy-start.30 = (s32[32]{0:T(128)}, s32[32]{0:T(128)S(1)}, u32[]{:S(2)}) copy-start(s32[32]{0:T(128)S(1)} %get-tuple-element.793) | copy-start | bytes 388
  62.3 14.1 %collective-permute-start.14 = (bf16[64,2048]{1,0:T(8,128)(2,1)S(1)}, bf16[64,2048]{1,0:T(8,128)(2,1)S(1)}, u32[]{:S(2)}, u32[]{:S(2)}) collective-permute-start(bf16[64,2048]{1,0:T(8,128)(2,1)S(1)} %collective-permute-done.12.refs_4_), channel_id=1, source_target_pairs={{0,4},{4,0},{8,12},{12,8},{1,5},{5,1},{9,13},{13,9},{2,6},{6,2},{1... | collective-permute-start | bytes 786440 | tf_op jit(solution)/shard_map/ppermute | solution.py:185
  70.8 11.8 %collective-permute-start.15 = (bf16[64,2048]{1,0:T(8,128)(2,1)S(1)}, bf16[64,2048]{1,0:T(8,128)(2,1)S(1)}, u32[]{:S(2)}, u32[]{:S(2)}) collective-permute-start(bf16[64,2048]{1,0:T(8,128)(2,1)S(1)} %collective-permute-done.13.refs_5_), channel_id=1, source_target_pairs={{0,4},{4,0},{8,12},{12,8},{1,5},{5,1},{9,13},{13,9},{2,6},{6,2},{1... | collective-permute-start | bytes 786440 | tf_op jit(solution)/shard_map/ppermute | solution.py:185
  76.5 18.2 %collective-permute-start.23 = (bf16[72,2048]{1,0:T(8,128)(2,1)S(1)}, bf16[72,2048]{1,0:T(8,128)(2,1)S(1)}, u32[]{:S(2)}, u32[]{:S(2)}) collective-permute-start(bf16[72,2048]{1,0:T(8,128)(2,1)S(1)} %convolution_convert_fusion.4), channel_id=1, source_target_pairs={{0,12},{4,8},{8,4},{12,0},{1,13},{5,9},{9,5},{13,1},{2,14},{6,10},... | collective-permute-start | bytes 884744 | tf_op jit(solution)/shard_map/ppermute | solution.py:185
  89.6 1.2 collective-permute-start.16
  90.9 3.7 %collective-permute-start.17 = (f32[32,128]{1,0:T(8,128)S(1)}, f32[32,128]{1,0:T(8,128)S(1)}, u32[]{:S(2)}, u32[]{:S(2)}) collective-permute-start(f32[32,128]{1,0:T(8,128)S(1)} %add.757), channel_id=1, source_target_pairs={{0,2},{1,3},{2,0},{3,1},{4,6},{5,7},{6,4},{7,5},{8,10},{9,11},{10,... | collective-permute-start | bytes 49160 | tf_op jit(solution)/shard_map/ppermute | solution.py:185
  94.6 33.2 %collective-permute-start.33 = (f32[64,128]{1,0:T(8,128)S(1)}, f32[64,128]{1,0:T(8,128)S(1)}, u32[]{:S(2)}, u32[]{:S(2)}) collective-permute-start(f32[64,128]{1,0:T(8,128)S(1)} %scores.8), channel_id=1, source_target_pairs={{0,1},{1,0},{2,3},{3,2},{4,5},{5,4},{6,7},{7,6},{8,9},{9,8},{10,11... | collective-permute-start | bytes 98312 | tf_op jit(solution)/shard_map/ppermute | solution.py:185
  101.0 7.8 %collective-permute-start.25 = (f32[44,128]{1,0:T(8,128)S(1)}, f32[44,128]{1,0:T(8,128)S(1)}, u32[]{:S(2)}, u32[]{:S(2)}) collective-permute-start(f32[44,128]{1,0:T(8,128)S(1)} %scores.7), channel_id=1, source_target_pairs={{0,1},{1,0},{2,3},{3,2},{4,5},{5,4},{6,7},{7,6},{8,9},{9,8},{10,11... | collective-permute-start | bytes 67592 | tf_op jit(solution)/shard_map/ppermute | solution.py:185
  106.1 21.8 %collective-permute-start.20 = (bf16[64,2048]{1,0:T(8,128)(2,1)S(1)}, bf16[64,2048]{1,0:T(8,128)(2,1)S(1)}, u32[]{:S(2)}, u32[]{:S(2)}) collective-permute-start(bf16[64,2048]{1,0:T(8,128)(2,1)S(1)} %get-tuple-element.478), channel_id=1, source_target_pairs={{0,4},{4,0},{8,12},{12,8},{1,5},{5,1},{9,13},{13,9},{2,6},{6,2},{1... | collective-permute-start | bytes 786440 | tf_op jit(solution)/shard_map/ppermute | solution.py:185
  108.7 22.2 %collective-permute-start.18 = (bf16[64,2048]{1,0:T(8,128)(2,1)S(1)}, bf16[64,2048]{1,0:T(8,128)(2,1)S(1)}, u32[]{:S(2)}, u32[]{:S(2)}) collective-permute-start(bf16[64,2048]{1,0:T(8,128)(2,1)S(1)} %get-tuple-element.476), channel_id=1, source_target_pairs={{0,4},{4,0},{8,12},{12,8},{1,5},{5,1},{9,13},{13,9},{2,6},{6,2},{1... | collective-permute-start | bytes 786440 | tf_op jit(solution)/shard_map/ppermute | solution.py:185
  108.8 23.5 %collective-permute-start.26 = (f32[44,128]{1,0:T(8,128)S(1)}, f32[44,128]{1,0:T(8,128)S(1)}, u32[]{:S(2)}, u32[]{:S(2)}) collective-permute-start(f32[44,128]{1,0:T(8,128)S(1)} %add.764), channel_id=1, source_target_pairs={{0,2},{1,3},{2,0},{3,1},{4,6},{5,7},{6,4},{7,5},{8,10},{9,11},{10,... | collective-permute-start | bytes 67592 | tf_op jit(solution)/shard_map/ppermute | solution.py:185
  127.9 63.1 %collective-permute-start.30 = (bf16[512,2048]{0,1:T(8,128)(2,1)}, bf16[512,2048]{0,1:T(8,128)(2,1)}, u32[]{:S(2)}, u32[]{:S(2)}) collective-permute-start(bf16[512,2048]{0,1:T(8,128)(2,1)} %fusion.47), channel_id=1, source_target_pairs={{0,1},{1,0},{2,3},{3,2},{4,5},{5,4},{6,7},{7,6},{8,9},{9,8},{10,11... | collective-permute-start | bytes 6291464 | tf_op jit(solution)/shard_map/ppermute | solution.py:185
  128.0 23.9 %collective-permute-start.11 = (s32[1]{0:T(128)}, s32[1]{0:T(128)}, u32[]{:S(2)}, u32[]{:S(2)}) collective-permute-start(s32[1]{0:T(128)} %bitcast.13), channel_id=1, source_target_pairs={{0,16},{16,0},{1,17},{17,1},{2,18},{18,2},{3,19},{19,3},{4,20},{20... | collective-permute-start | bytes 20 | tf_op jit(solution)/shard_map/ppermute | solution.py:185
  130.9 21.4 %collective-permute-start.34 = (f32[64,128]{1,0:T(8,128)S(1)}, f32[64,128]{1,0:T(8,128)S(1)}, u32[]{:S(2)}, u32[]{:S(2)}) collective-permute-start(f32[64,128]{1,0:T(8,128)S(1)} %add.772), channel_id=1, source_target_pairs={{0,2},{1,3},{2,0},{3,1},{4,6},{5,7},{6,4},{7,5},{8,10},{9,11},{10,... | collective-permute-start | bytes 98312 | tf_op jit(solution)/shard_map/ppermute | solution.py:185
  132.3 31.7 %collective-permute-start.21 = (bf16[64,2048]{1,0:T(8,128)(2,1)S(1)}, bf16[64,2048]{1,0:T(8,128)(2,1)S(1)}, u32[]{:S(2)}, u32[]{:S(2)}) collective-permute-start(bf16[64,2048]{1,0:T(8,128)(2,1)S(1)} %add.760), channel_id=1, source_target_pairs={{0,12},{4,8},{8,4},{12,0},{1,13},{5,9},{9,5},{13,1},{2,14},{6,10},... | collective-permute-start | bytes 786440 | tf_op jit(solution)/shard_map/ppermute | solution.py:185
  146.0 46.9 %collective-permute-start.32 = (bf16[512,2048]{0,1:T(8,128)(2,1)}, bf16[512,2048]{0,1:T(8,128)(2,1)}, u32[]{:S(2)}, u32[]{:S(2)}) collective-permute-start(bf16[512,2048]{0,1:T(8,128)(2,1)} %fusion.31), channel_id=1, source_target_pairs={{0,2},{1,3},{2,0},{3,1},{4,6},{5,7},{6,4},{7,5},{8,10},{9,11},{10,... | collective-permute-start | bytes 6291464 | tf_op jit(solution)/shard_map/ppermute | solution.py:185
  151.8 14.3 %collective-permute-start.19 = (bf16[64,2048]{1,0:T(8,128)(2,1)}, bf16[64,2048]{1,0:T(8,128)(2,1)}, u32[]{:S(2)}, u32[]{:S(2)}) collective-permute-start(bf16[64,2048]{1,0:T(8,128)(2,1)} %add.759), channel_id=1, source_target_pairs={{0,8},{4,12},{8,0},{12,4},{1,9},{5,13},{9,1},{13,5},{2,10},{6,14},... | collective-permute-start | bytes 786440 | tf_op jit(solution)/shard_map/ppermute | solution.py:185
  152.3 38.7 %collective-permute-start.29 = (bf16[208,2048]{1,0:T(8,128)(2,1)S(1)}, bf16[208,2048]{1,0:T(8,128)(2,1)S(1)}, u32[]{:S(2)}, u32[]{:S(2)}) collective-permute-start(bf16[208,2048]{1,0:T(8,128)(2,1)S(1)} %get-tuple-element.484), channel_id=1, source_target_pairs={{0,4},{4,0},{8,12},{12,8},{1,5},{5,1},{9,13},{13,9},{2,6},{6,2},{1... | collective-permute-start | bytes 2555912 | tf_op jit(solution)/shard_map/ppermute | solution.py:185
  164.0 19.9 %collective-permute-start.27 = (bf16[72,2048]{1,0:T(8,128)(2,1)S(1)}, bf16[72,2048]{1,0:T(8,128)(2,1)S(1)}, u32[]{:S(2)}, u32[]{:S(2)}) collective-permute-start(bf16[72,2048]{1,0:T(8,128)(2,1)S(1)} %get-tuple-element.482), channel_id=1, source_target_pairs={{0,8},{4,12},{8,0},{12,4},{1,9},{5,13},{9,1},{13,5},{2,10},{6,14},... | collective-permute-start | bytes 884744 | tf_op jit(solution)/shard_map/ppermute | solution.py:185
  166.1 24.9 %collective-permute-start.28 = (bf16[72,2048]{1,0:T(8,128)(2,1)S(1)}, bf16[72,2048]{1,0:T(8,128)(2,1)S(1)}, u32[]{:S(2)}, u32[]{:S(2)}) collective-permute-start(bf16[72,2048]{1,0:T(8,128)(2,1)S(1)} %get-tuple-element.483), channel_id=1, source_target_pairs={{0,12},{4,8},{8,4},{12,0},{1,13},{5,9},{9,5},{13,1},{2,14},{6,10},... | collective-permute-start | bytes 884744 | tf_op jit(solution)/shard_map/ppermute | solution.py:185
  169.0 25.3 %copy-start.21 = (s32[32]{0:T(128)S(1)}, s32[32]{0:T(128)}, u32[]{:S(2)}) copy-start(s32[32]{0:T(128)} %copy-done.20) | copy-start | bytes 388
  169.0 25.3 %copy-start.23 = (s32[32]{0:T(128)S(1)}, s32[32]{0:T(128)}, u32[]{:S(2)}) copy-start(s32[32]{0:T(128)} %copy-done.22) | copy-start | bytes 388
  (29 other events, 236.7 us)

commit v2 on v1

v2 whole, which is shorter than its diff:
```python
import functools

import jax
import jax.numpy as jnp
from jax import lax
from jax.experimental import pallas as pl
from jax.experimental.pallas import tpu as pltpu
from jax.sharding import PartitionSpec as P

NEAR = 208
OWN = 72
SHARED = 64
ROUND = 64
VMEM = 48 * 2**20
FREE = pl.CostEstimate(flops=0, bytes_accessed=0, transcendentals=0)


def group_of(shape):
    return lax.broadcasted_iota(jnp.int32, shape, 1) // 16


def row_of(shape):
    return lax.broadcasted_iota(jnp.int32, shape, 0) % 8


def fold(v):
    for shift in (64, 32, 16):
        v = v + pltpu.roll(v, shift, axis=1)
    return v


def score_kernel(sizes, *refs):
    m = len(sizes)
    slots, got, a_ref, out_ref, acc = refs[:m], refs[m:2 * m], refs[2 * m], refs[2 * m + 1], refs[2 * m + 2]
    g = pl.program_id(0)
    per = a_ref.shape[0] // 16

    @pl.when(g == 0)
    def _():
        acc[...] = jnp.zeros_like(acc)

    off = 0
    for i, n in enumerate(sizes):
        s = lax.dot_general(
            got[i][...], a_ref[...], (((1,), (1,)), ((), ())), preferred_element_type=jnp.float32
        )
        s = jnp.where(group_of(s.shape) + g * per == slots[i][...], s, 0.0)
        v = s[:, :128]
        for c in range(128, s.shape[1], 128):
            v = v + s[:, c:c + 128]
        acc[off:off + n, :] += v
        off += n

    @pl.when(g == pl.num_programs(0) - 1)
    def _():
        off = 0
        for n in sizes:
            v = fold(acc[off:off + n, :])
            v = jnp.where(group_of(v.shape) == row_of(v.shape), v, 0.0)
            out_ref[off // 8:(off + n) // 8, :] = jnp.sum(v.reshape(n // 8, 8, 128), axis=1)
            off += n


def scores(slots, got, store):
    sizes = tuple(v.shape[0] for v in got)
    total, width = sum(sizes), store.shape[1]
    blk = 256
    whole = lambda v: pl.BlockSpec(v.shape, lambda g: (0, 0))
    return pl.pallas_call(
        functools.partial(score_kernel, sizes),
        grid=(store.shape[0] // blk,),
        in_specs=[whole(v) for v in slots] + [whole(v) for v in got]
        + [pl.BlockSpec((blk, width), lambda g: (g, 0))],
        out_specs=pl.BlockSpec((total // 8, 128), lambda g: (0, 0)),
        out_shape=jax.ShapeDtypeStruct((total // 8, 128), jnp.float32),
        scratch_shapes=[pltpu.VMEM((total, 128), jnp.float32)],
        compiler_params=pltpu.CompilerParams(vmem_limit_bytes=VMEM),
        cost_estimate=FREE,
        name="scores",
    )(*slots, *got, store)


def delta_kernel(sizes, *refs):
    m = len(sizes)
    slots, packed, b_ref, outs, spread = refs[:m], refs[m], refs[m + 1], refs[m + 2:2 * m + 2], refs[2 * m + 2:]

    @pl.when(pl.program_id(0) == 0)
    def _():
        off = 0
        for i, n in enumerate(sizes):
            v = packed[off // 8:(off + n) // 8, :]
            v = jnp.broadcast_to(v[:, None, :], (n // 8, 8, 128)).reshape(n, 128)
            group = group_of(v.shape)
            v = fold(jnp.where(group == row_of(v.shape), v, 0.0))
            for c in range(b_ref.shape[0] // 128):
                hit = group + c * 8 == slots[i][...]
                spread[i][:, c * 128:(c + 1) * 128] = jnp.where(hit, v, 0.0).astype(jnp.bfloat16)
            off += n

    for i in range(m):
        outs[i][...] = jnp.dot(
            spread[i][...], b_ref[...], preferred_element_type=jnp.float32
        ).astype(jnp.bfloat16)


def deltas(slots, packed, store):
    sizes = tuple(v.shape[0] for v in slots)
    depth, width = store.shape
    cols = width // 4
    whole = lambda v: pl.BlockSpec(v.shape, lambda g: (0, 0))
    return pl.pallas_call(
        functools.partial(delta_kernel, sizes),
        grid=(width // cols,),
        in_specs=[whole(v) for v in slots] + [whole(packed)]
        + [pl.BlockSpec((depth, cols), lambda g: (0, g))],
        out_specs=[pl.BlockSpec((n, cols), lambda g: (0, g)) for n in sizes],
        out_shape=[jax.ShapeDtypeStruct((n, width), jnp.bfloat16) for n in sizes],
        scratch_shapes=[pltpu.VMEM((n, depth), jnp.bfloat16) for n in sizes],
        compiler_params=pltpu.CompilerParams(vmem_limit_bytes=VMEM),
        cost_estimate=FREE,
        name="deltas",
    )(*slots, packed, store)


def finish_kernel(m, a, row_ref, *refs):
    codes, back, adds, out_ref = refs[:m], refs[m:2 * m], refs[2 * m:2 * m + a], refs[2 * m + a]
    total = adds[0][...].astype(jnp.float32)
    for v in adds[1:]:
        total += v[...].astype(jnp.float32)
    for code, b in zip(codes, back):
        put = jnp.where(row_ref[...] == code[...], 1.0, 0.0).astype(jnp.bfloat16)
        total += jnp.dot(put, b[...], preferred_element_type=jnp.float32)
    out_ref[...] = total.astype(out_ref.dtype)


def finish(row_code, codes, back, adds):
    rows, width = adds[0].shape
    cols = width // 4
    whole = lambda v: pl.BlockSpec(v.shape, lambda g: (0, 0))
    part = lambda v: pl.BlockSpec((v.shape[0], cols), lambda g: (0, g))
    return pl.pallas_call(
        functools.partial(finish_kernel, len(codes), len(adds)),
        grid=(width // cols,),
        in_specs=[whole(row_code)] + [whole(v) for v in codes] + [part(v) for v in back] + [part(v) for v in adds],
        out_specs=pl.BlockSpec((rows, cols), lambda g: (0, g)),
        out_shape=jax.ShapeDtypeStruct((rows, width), jnp.bfloat16),
        compiler_params=pltpu.CompilerParams(vmem_limit_bytes=VMEM),
        name="finish",
    )(row_code, *codes, *back, *adds)


def column(row):
    n = row.shape[1]
    eye = lax.broadcasted_iota(jnp.int32, (n, n), 0) == lax.broadcasted_iota(jnp.int32, (n, n), 1)
    return jnp.sum(jnp.where(eye, jnp.broadcast_to(row, (n, n)), 0), axis=1, keepdims=True)


def row(col):
    n = col.shape[0]
    eye = lax.broadcasted_iota(jnp.int32, (n, n), 0) == lax.broadcasted_iota(jnp.int32, (n, n), 1)
    return jnp.sum(jnp.where(eye, jnp.broadcast_to(col, (n, n)), 0), axis=0, keepdims=True)


def segments(pos, alive, device, shift):
    n = pos.shape[1]
    dist = (pos >> shift) ^ device
    i = lax.broadcasted_iota(jnp.int32, (n, n), 0)
    j = lax.broadcasted_iota(jnp.int32, (n, n), 1)
    before = (column(dist) == dist) & (i < j)
    start = jnp.sum(jnp.where(before, column(alive), 0), axis=0, keepdims=True)
    return dist, start


def total(dist, alive, j):
    return jnp.sum(jnp.where(dist == j, alive, 0), axis=1, keepdims=True)


def over_of(dist, alive, j):
    return jnp.maximum(total(dist, alive, j - j % 2) - OWN, 0)


def iota_of(n, axis):
    return lax.broadcasted_iota(jnp.int32, (n, 1) if axis == 0 else (1, n), axis)


def near_code(big, axis):
    return big + iota_of(NEAR, axis)


def own_code(big, j, axis):
    return j * big + iota_of(OWN, axis)


def shared_code(big, j, over, axis):
    f = iota_of(SHARED, axis) + (j % 2) * SHARED
    even = j - j % 2
    return OWN + jnp.where(f < over, even * big + f, (even + 1) * big + f - over)


def far_code(big, j, over, axis):
    f = iota_of(SHARED + OWN, axis)
    g = f + (j % 2) * SHARED
    even = j - j % 2
    code = OWN + jnp.where(g < over, even * big + g, (even + 1) * big + g - over)
    return jnp.where(f < SHARED, code, j * big + f - SHARED)


def pack_kernel(n_dp, seg_len, shift, me_ref, ids_ref, lives_ref, index_ref, x_ref,
                table_ref, row_ref, self_ref, *outs):
    me = me_ref[0]
    count, rows = ids_ref.shape[1], x_ref.shape[0]
    big = 2 * rows
    lives = lives_ref[...]
    index = index_ref[...]
    hit = column(ids_ref[...]) == lax.broadcasted_iota(jnp.int32, (count, index.shape[1]), 1)
    pos = row(jnp.sum(jnp.where(hit, index, 0), axis=1, keepdims=True))
    table_ref[0:1, :] = pos
    table_ref[1:2, :] = lives
    dist, start = segments(pos, lives, me, shift)
    code = dist * big + start
    slot = jnp.where(dist == 0, pos & ((1 << shift) - 1), -1)

    def spread(value, axis):
        shape = (count, rows) if axis == 1 else (rows, count)
        r = lax.broadcasted_iota(jnp.int32, shape, axis)
        seg = lax.broadcasted_iota(jnp.int32, shape, 1 - axis)
        v = column(value) if axis == 1 else value
        return jnp.sum(jnp.where(r // seg_len == seg, v, 0), axis=1 - axis, keepdims=True)

    def rows_code(axis):
        lane = iota_of(rows, axis) % seg_len
        return jnp.where(lane < spread(lives, axis), spread(code, axis) + lane, -1)

    by_row = rows_code(0)
    row_ref[...] = by_row
    self_ref[...] = jnp.where(by_row >= 0, spread(slot, 0), -1)
    by_lane = rows_code(1)

    far = range(2, n_dp)
    codes = [far_code(big, j, over_of(dist, lives, j), 0) for j in far] + [near_code(big, 0)]
    m = len(codes)
    for c, out in zip(codes, outs[:m]):
        pick = jnp.where(c == by_lane, 1.0, 0.0).astype(jnp.bfloat16)
        out[...] = jnp.dot(pick, x_ref[...], preferred_element_type=jnp.float32).astype(jnp.bfloat16)
    lanes = [shared_code(big, j, over_of(dist, lives, j), 1) for j in far]
    lanes += [own_code(big, j, 1) for j in far] + [near_code(big, 1)]
    for c, out in zip(lanes, outs[m:]):
        out[...] = c


def vmem(count):
    return [pl.BlockSpec(memory_space=pltpu.VMEM) for _ in range(count)]


def packs(me, ids, lives, index, x, n_dp, seg_len, shift):
    count, (rows, width) = ids.shape[1], x.shape
    sizes = [SHARED + OWN] * (n_dp - 2) + [NEAR]
    parts = [SHARED] * (n_dp - 2) + [OWN] * (n_dp - 2) + [NEAR]
    shapes = [((2, count), jnp.int32), ((rows, 1), jnp.int32), ((rows, 1), jnp.int32)]
    shapes += [((n, width), jnp.bfloat16) for n in sizes] + [((1, n), jnp.int32) for n in parts]
    return pl.pallas_call(
        functools.partial(pack_kernel, n_dp, seg_len, shift),
        in_specs=[pl.BlockSpec(memory_space=pltpu.SMEM)] + vmem(4),
        out_specs=vmem(len(shapes)),
        out_shape=[jax.ShapeDtypeStruct(*v) for v in shapes],
        compiler_params=pltpu.CompilerParams(vmem_limit_bytes=VMEM),
        cost_estimate=FREE,
        name="pack",
    )(me, ids, lives, index, x)


def slots_kernel(n_dp, rows, shift, me_ref, *refs):
    tables, outs, left_ref = refs[:n_dp], refs[n_dp:-1], refs[-1]
    big = 2 * rows
    me = me_ref[0]
    plans, left = [], None
    for k in range(n_dp):
        pos, alive = tables[k][0:1, :], tables[k][1:2, :]
        dist, start = segments(pos, alive, me ^ k, shift)
        plans.append((pos, alive, dist, start))
        rest = [total(dist, alive, 1) - NEAR]
        for j in range(2, n_dp):
            held = OWN + 2 * SHARED if j % 2 == 0 else OWN + jnp.maximum(2 * SHARED - over_of(dist, alive, j), 0)
            rest.append(total(dist, alive, j) - held)
        for v in rest:
            left = v if left is None else jnp.maximum(left, v)
    left_ref[...] = left

    def slots_of(k, code, out):
        pos, alive, dist, start = plans[k]
        seg = dist * big + start
        hit = (code >= seg) & (code < seg + alive) & (dist == k)
        out[...] = jnp.max(jnp.where(hit, pos & ((1 << shift) - 1), -1), axis=1, keepdims=True)

    far = range(2, n_dp)
    over = [over_of(p[2], p[1], k) for k, p in enumerate(plans)]
    todo = [(j ^ 1, shared_code(big, j, over_of(plans[j ^ 1][2], plans[j ^ 1][1], j), 0)) for j in far]
    todo += [(j, shared_code(big, j, over[j], 0)) for j in far]
    todo += [(j, own_code(big, j, 0)) for j in far]
    todo += [(j, far_code(big, j, over[j], 0)) for j in far]
    todo += [(1, near_code(big, 0))]
    for (k, code), out in zip(todo, outs):
        slots_of(k, code, out)


def slots(me, tables, rows, shift):
    n_dp = len(tables)
    sizes = [n for n in (SHARED, SHARED, OWN, SHARED + OWN) for _ in range(2, n_dp)] + [NEAR]
    shapes = [(n, 1) for n in sizes] + [(1, 1)]
    return pl.pallas_call(
        functools.partial(slots_kernel, n_dp, rows, shift),
        in_specs=[pl.BlockSpec(memory_space=pltpu.SMEM)] + vmem(n_dp),
        out_specs=vmem(len(shapes)),
        out_shape=[jax.ShapeDtypeStruct(v, jnp.int32) for v in shapes],
        cost_estimate=FREE,
        name="slots",
    )(me, *tables)


def share_kernel(at_ref, x_ref, w_ref, *refs):
    v = jnp.dot(x_ref[...], w_ref[...], preferred_element_type=jnp.float32)
    for r in refs[:-1]:
        v += r[...].astype(jnp.float32)
    refs[-1][...] = v.astype(jnp.bfloat16)


def share(at, x, weight, cols, adds):
    rows, depth = x.shape
    tile = min(512, cols)
    part = pl.BlockSpec((rows, tile), lambda g, at: (0, g))
    return pl.pallas_call(
        share_kernel,
        grid_spec=pltpu.PrefetchScalarGridSpec(
            num_scalar_prefetch=1,
            grid=(cols // tile,),
            in_specs=[
                pl.BlockSpec((rows, depth), lambda g, at: (0, 0)),
                pl.BlockSpec((depth, tile), lambda g, at: (0, at[0] * (cols // tile) + g)),
            ] + [part] * len(adds),
            out_specs=part,
        ),
        out_shape=jax.ShapeDtypeStruct((rows, cols), jnp.bfloat16),
        compiler_params=pltpu.CompilerParams(vmem_limit_bytes=VMEM),
        cost_estimate=FREE,
        name="share",
    )(at, x, weight, *adds)


def per_device(
    attention_output,
    output_projection_weight,
    shrink_matrix_store,
    expand_matrix_store,
    segment_adapter,
    segment_live_rows,
    adapter_store_index,
):
    steps, rows_dev, width = attention_output.shape
    seg_count = segment_adapter.shape[1]
    seg_len = rows_dev // seg_count
    store, rank, _ = shrink_matrix_store.shape
    n_dp, n_tp = lax.axis_size("dp"), lax.axis_size("tp")
    me = lax.axis_index("dp").reshape(1)
    rows = steps * rows_dev
    count = steps * seg_count
    shift = store.bit_length() - 1
    big = 2 * rows
    far = range(2, n_dp)

    x = attention_output.reshape(rows, width)
    shrink_store = shrink_matrix_store.reshape(store * rank, width)
    expand_store = expand_matrix_store.reshape(store * rank, width)
    weight = output_projection_weight

    def swap(v, axis, k):
        n = lax.axis_size(axis)
        return lax.ppermute(v, axis, [(i, i ^ k) for i in range(n)])

    def butterfly(v, axis, op):
        k = 1
        while k < lax.axis_size(axis):
            v = op(v, swap(v, axis, k))
            k *= 2
        return v

    def answer(slots, parts, got):
        part = butterfly(scores(slots, got, shrink_store), "tp", jnp.add)
        return deltas(parts, part, expand_store)

    packed = list(packs(
        me,
        segment_adapter.reshape(1, count),
        segment_live_rows.reshape(1, count),
        adapter_store_index.reshape(1, -1),
        x, n_dp, seg_len, shift,
    ))
    table, row_code, self_slots = packed[:3]
    m = len(far)
    out_far, out_near, codes = packed[3:3 + m], packed[3 + m], packed[4 + m:]

    in_far = [swap(v, "dp", j) for v, j in zip(out_far, far)]
    in_near = swap(out_near, "dp", 1)
    tables = [table] + [swap(table, "dp", k) for k in range(1, n_dp)]

    at = lax.axis_index("tp").reshape(1)
    cols = weight.shape[1] // n_tp
    at, _ = lax.optimization_barrier((at, table))
    adds = {k: [] for k in range(n_tp)}
    bit = 1
    while bit < n_tp:
        for k in sorted((k for k in adds if k & bit), reverse=True):
            v = share(at ^ k, x, weight, cols, adds.pop(k))
            adds[k ^ bit].append(swap(v, "tp", bit))
        bit *= 2
    base = [share(at, x, weight, cols, adds[0][:1])] + adds[0][1:]

    found = list(slots(me, tables, rows, shift))
    left = butterfly(found[-1], "rep", jnp.maximum)[0, 0]
    relay_slots, shared_slots, own_slots, far_slots = (found[i * m:(i + 1) * m] for i in range(4))
    near_slots = found[4 * m]

    (self_delta,) = answer([self_slots], [self_slots], [x])
    base[0], self_delta, far_slots = lax.optimization_barrier((base[0], self_delta, far_slots))

    in_relay = [swap(v[:SHARED], "dp", 1) for v in in_far]
    split = [v for pair in zip(shared_slots, own_slots) for v in pair] + [near_slots]
    direct = answer(far_slots + [near_slots], split, in_far + [in_near])
    relayed = answer(relay_slots, relay_slots, in_relay)
    back_shared = [direct[2 * i] + swap(relayed[i], "dp", 1) for i in range(m)]
    back_shared = [swap(v, "dp", j) for v, j in zip(back_shared, far)]
    back_own = [swap(direct[2 * i + 1], "dp", j) for i, j in enumerate(far)]
    back_near = swap(direct[-1], "dp", 1)

    back = back_shared + back_own + [back_near]
    adds = base + [self_delta]

    def layout(k):
        pos, alive = tables[k][0], tables[k][1]
        dist = (pos >> shift) ^ (me[0] ^ k)
        order = jnp.arange(count, dtype=jnp.int32)
        before = (dist[:, None] == dist[None, :]) & (order[:, None] > order[None, :])
        start = jnp.sum(jnp.where(before, alive[None, :], 0), axis=1)
        held = [None, jnp.int32(NEAR)]
        for j in range(2, n_dp, 2):
            extra = jnp.maximum(jnp.sum(jnp.where(dist == j, alive, 0)) - OWN, 0)
            held += [jnp.int32(OWN + 2 * SHARED), OWN + jnp.maximum(2 * SHARED - extra, 0)]
        return dist, start, alive, pos & (store - 1), held

    def rest():
        lay = [layout(k) for k in range(n_dp)]

        def code_of(k, j, low):
            return j * big + lay[k][4][j] + low + jnp.arange(ROUND, dtype=jnp.int32)

        def slots_of(k, code):
            dist, start, alive, slot, _ = lay[k]
            seg = dist * big + start
            hit = (code[:, None] >= seg[None, :]) & (code[:, None] < (seg + alive)[None, :])
            hit = hit & (dist == k)[None, :]
            return jnp.max(jnp.where(hit, slot[None, :], -1), axis=1, keepdims=True)

        def body(i, extra):
            low = i * ROUND
            got, found = [], []
            for j in range(1, n_dp):
                pick = (code_of(0, j, low)[:, None] == row_code.reshape(1, rows)).astype(jnp.bfloat16)
                v = jnp.dot(pick, x, preferred_element_type=jnp.float32).astype(jnp.bfloat16)
                got.append(swap(v, "dp", j))
                found.append(slots_of(j, code_of(j, j, low)))
            for j, v in zip(range(1, n_dp), answer(found, found, got)):
                put = (row_code == code_of(0, j, low)[None, :]).astype(jnp.bfloat16)
                extra = extra + jnp.dot(put, swap(v, "dp", j), preferred_element_type=jnp.float32)
            return extra

        rounds = (left + ROUND - 1) // ROUND
        extra = lax.fori_loop(0, rounds, body, jnp.zeros((rows, width), jnp.float32))
        return finish(row_code, codes, back, adds + [extra])

    out = lax.cond(left > 0, rest, lambda: finish(row_code, codes, back, adds))
    return out.reshape(steps, rows_dev, width)


def solution(mesh):
    return jax.shard_map(
        per_device,
        mesh=mesh,
        in_specs=(
            P(None, ("rep", "dp"), "tp"),
            P("tp", None),
            P("dp", None, "tp"),
            P("dp", None, "tp"),
            P(None, ("rep", "dp")),
            P(None, ("rep", "dp")),
            P("rep"),
        ),
        out_specs=P(None, ("rep", "dp"), "tp"),
        check_vma=False,
    )
```

time: 216 us -> 233 us (1.079)
  waiting for transfers between devices: 29.1 us -> 94.4 us
  matrix products: 46.5 us -> 0 us
  Pallas kernels: 39.8 us -> 75.2 us
  local copies, waits for them, and re-layouts: 22.4 us -> 5.01 us
  other arithmetic: 17.5 us -> 0.85 us
  between operations: 11 us -> 1.5 us
  starting transfers between devices: 48.5 us -> 54.8 us
    ppermute x27 -> x25, waiting for transfers between devices: 29.1 us -> 94.4 us  [swap(): return lax.ppermute(v, axis, [(i, i ^ k) for i in range(n)])]
    dot_general x9 -> x0, matrix products: 46.5 us -> none  [the longest x4 39.1 us: share(): jnp.dot(x, w, preferred_element_type=jnp.float32).astype(jnp.bfloat16)]
    pallas_call x0 -> x6, Pallas kernels: none -> 37.2 us  [the longest x4 30.9 us: share(): pl.pallas_call(share_kernel, grid_spec=pltpu.PrefetchScalarGridSpec(num_s...]
    another operation x5 -> x0, local copies, waits for them, and re-layouts: 11.7 us -> none
    reduce_sum x9 -> x0, other arithmetic: 8.88 us -> none  [the longest x4 7.31 us: layout(): totals = [jnp.sum(jnp.where(dist == j, alive, 0)) for j in range(n_dp)]]
    ppermute x27 -> x25, starting transfers between devices: 48.5 us -> 54.8 us  [swap(): return lax.ppermute(v, axis, [(i, i ^ k) for i in range(n)])]
    pallas_call x3, Pallas kernels: 18.5 us -> 16 us  [scores(): pl.pallas_call(functools.partial(score_kernel, sizes), grid=(store.shape[...]
  transfers between devices with their start and end apart: 27 -> 25, of which waited for: 8 -> 12; matrix products, arithmetic and copies ran while one was open for 31% -> 1% of each run, Pallas kernels for 16% -> 25%
where the time goes in v2:
time: 233 us; the launch traced here: 232 us
  waiting for transfers between devices  94.4 us (41%)
  Pallas kernels  75.2 us (32%)
  starting transfers between devices  54.8 us (24%)
  local copies, waits for them, and re-layouts  5.01 us (2%)
    ppermute x25, waiting for transfers between devices, swap(): return lax.ppermute(v, axis, [(i, i ^ k) for i in range(n)])  94.4 us
    ppermute x25, starting transfers between devices, swap(): return lax.ppermute(v, axis, [(i, i ^ k) for i in range(n)])  54.8 us
    pallas_call x4, Pallas kernels, share(): pl.pallas_call(share_kernel, grid_spec=pltpu.PrefetchScalarGridSpec(num_s...  30.9 us
    pallas_call x3, Pallas kernels, scores(): pl.pallas_call(functools.partial(score_kernel, sizes), grid=(store.shape[...  16 us
    pallas_call x3, Pallas kernels, deltas(): pl.pallas_call(functools.partial(delta_kernel, sizes), grid=(width // col...  15.6 us
    pallas_call x1, Pallas kernels, finish(): pl.pallas_call(functools.partial(finish_kernel, len(codes), len(adds)), g...  6.46 us
  transfers between devices with their start and end apart: 25, of which 12 were waited for; matrix products, arithmetic and copies ran while one was open for 1% of the time, Pallas kernels for 25%

profile of v2, /device:TPU:0, one launch (start us, length us, event | category | flops | bytes accessed | tf_op | source)
XLA Modules:
  0.0 232.0 jit_solution(2987073826673261768)
XLA Ops:
  2.2 4.4 %pack.1 = (s32[2,32]{1,0:T(2,128)S(1)}, s32[512,1]{1,0:T(8,128)}, s32[512,1]{1,0:T(8,128)S(1)}, bf16[136,2048]{1,0:T(8,128)(2,1)S(1)}, bf16[136,2048]{1,0:T(8,12...) custom-call(s32[1]{0:T(128)} %bitcast.15.me_ref, ...), custom_call_target="tpu_custom_call" | custom-call | tf_op jit(solution)/shard_map/pack/pallas_call | solution.py:261
  6.6 7.1 %share.6 = bf16[512,2048]{1,0:T(8,128)(2,1)S(1)} custom-call(s32[1]{0:T(128)S(6)} %xor.69.at_ref, bf16[512,2048]{1,0:T(8,128)(2,1)S(1)} %bitcast.62, bf16[2048,8192]{1,0:T(8,128)(2,1)} %w_ref.7), custom_call_target="tpu_custom_call" | custom-call | tf_op jit(solution)/shard_map/share/pallas_call | solution.py:331
  14.3 7.1 %share.4 = bf16[512,2048]{1,0:T(8,128)(2,1)S(1)} custom-call(s32[1]{0:T(128)S(6)} %xor.67.at_ref, bf16[512,2048]{1,0:T(8,128)(2,1)S(1)} %bitcast.63, bf16[2048,8192]{1,0:T(8,128)(2,1)} %w_ref.7), custom_call_target="tpu_custom_call" | custom-call | tf_op jit(solution)/shard_map/share/pallas_call | solution.py:331
  21.5 8.2 %share.7 = bf16[512,2048]{1,0:T(8,128)(2,1)} custom-call(s32[1]{0:T(128)S(6)} %xor.68.at_ref, bf16[512,2048]{1,0:T(8,128)(2,1)S(1)} %bitcast.64, bf16[2048,8192]{1,0:T(8,128)(2,1)} %w_ref.7, bf16[512,2048]{1,0:T(8,128)(2,1)S(1)} %collective-permute-done.31.refs_0_), custom_call_target="tpu_custom_call" | custom-call | tf_op jit(solution)/shard_map/share/pallas_call | solution.py:331
  29.7 3.0 %collective-permute-start.32 = (bf16[512,2048]{1,0:T(8,128)(2,1)}, bf16[512,2048]{1,0:T(8,128)(2,1)}, u32[]{:S(2)}, u32[]{:S(2)}) collective-permute-start(bf16[512,2048]{1,0:T(8,128)(2,1)} %share.7), channel_id=1, source_target_pairs={{0,2},{1,3},{2,0},{3,1},{4,6},{5,7},{6,4},{7,5},{8,10},{9,11},{10,... | collective-permute-start | bytes 6291464 | tf_op jit(solution)/shard_map/ppermute | solution.py:377
  34.2 2.5 %collective-permute-start.10 = (s32[2,32]{1,0:T(2,128)S(1)}, s32[2,32]{1,0:T(2,128)S(1)}, u32[]{:S(2)}, u32[]{:S(2)}) collective-permute-start(s32[2,32]{1,0:T(2,128)S(1)} %get-tuple-element.396.refs_0_), channel_id=1, source_target_pairs={{0,12},{4,8},{8,4},{12,0},{1,13},{5,9},{9,5},{13,1},{2,14},{6,10},... | collective-permute-start | bytes 776 | tf_op jit(solution)/shard_map/ppermute | solution.py:377
  36.7 5.2 %scores.6 = f32[64,128]{1,0:T(8,128)S(1)} custom-call(s32[512,1]{1,0:T(8,128)S(1)} %get-tuple-element.410.refs_0_, bf16[512,2048]{1,0:T(8,128)(2,1)S(1)} %bitcast.65, bf16[1024,2048]{1,0:T(8,128)(2,1)} %bitcast.68), custom_call_target="tpu_custom_call" | custom-call | tf_op jit(solution)/shard_map/scores/pallas_call | solution.py:69
  42.0 13.5 %collective-permute-done.10.refs_3_ = s32[2,32]{1,0:T(2,128)S(1)} collective-permute-done((s32[2,32]{1,0:T(2,128)S(1)}, s32[2,32]{1,0:T(2,128)S(1)}, u32[]{:S(2)}, u32[]{:S(2)}) %collective-permute-start.10) | collective-permute-done | bytes 288 | tf_op jit(solution)/shard_map/ppermute | solution.py:377
  55.5 4.6 %collective-permute-done.9.refs_2_ = s32[2,32]{1,0:T(2,128)S(1)} collective-permute-done((s32[2,32]{1,0:T(2,128)S(1)}, s32[2,32]{1,0:T(2,128)S(1)}, u32[]{:S(2)}, u32[]{:S(2)}) %collective-permute-start.9) | collective-permute-done | bytes 288 | tf_op jit(solution)/shard_map/ppermute | solution.py:377
  61.4 34.2 %collective-permute-done.15.refs_3_ = bf16[136,2048]{1,0:T(8,128)(2,1)S(1)} collective-permute-done((bf16[136,2048]{1,0:T(8,128)(2,1)S(1)}, bf16[136,2048]{1,0:T(8,128)(2,1)S(1)}, u32[]{:S(2)}, u32[]{:S(2)}) %collective-permute-start.15) | collective-permute-done | bytes 557088 | tf_op jit(solution)/shard_map/ppermute | solution.py:377
  96.1 11.9 %collective-permute-start.8 = (s32[2,32]{1,0:T(2,128)S(1)}, s32[2,32]{1,0:T(2,128)S(1)}, u32[]{:S(2)}, u32[]{:S(2)}) collective-permute-start(s32[2,32]{1,0:T(2,128)S(1)} %get-tuple-element.396.refs_0_), channel_id=1, source_target_pairs={{0,4},{4,0},{8,12},{12,8},{1,5},{5,1},{9,13},{13,9},{2,6},{6,2},{1... | collective-permute-start | bytes 776 | tf_op jit(solution)/shard_map/ppermute | solution.py:377
  109.5 2.0 collective-permute-start.20
  111.6 1.9 slots.1
  113.5 6.8 %deltas.6 = bf16[512,2048]{1,0:T(8,128)(2,1)} custom-call(s32[512,1]{1,0:T(8,128)S(1)} %get-tuple-element.410.refs_0_, f32[64,128]{1,0:T(8,128)S(1)} %add.247.refs_1_, bf16[1024,2048]{1,0:T(8,128)(2,1)} %bitcast.72), custom_call_target="tpu_custom_call" | custom-call | tf_op jit(solution)/shard_map/deltas/pallas_call | solution.py:111
  120.3 8.5 %share.5 = bf16[512,2048]{1,0:T(8,128)(2,1)} custom-call(s32[1]{0:T(128)} %bitcast.19.at_ref, bf16[512,2048]{1,0:T(8,128)(2,1)S(1)} %bitcast.66, bf16[2048,8192]{1,0:T(8,128)(2,1)} %w_ref.7, bf16[512,2048]{1,0:T(8,128)(2,1)} %collective-permute-done.12.refs_0_), custom_call_target="tpu_custom_call" | custom-call | tf_op jit(solution)/shard_map/share/pallas_call | solution.py:331
  128.8 6.5 %scores.7 = f32[60,128]{1,0:T(8,128)S(1)} custom-call(s32[136,1]{1,0:T(8,128)S(1)} %copy-done.3, s32[136,1]{1,0:T(8,128)S(1)} %copy-done.4, s32[208,1]{1,0:T(8,128)S(1)} %copy-done, bf16[136,2048]{1,0:T(8,128)(2,1)S(1)} %collective-permute-done.15.refs_3_, bf16[136,2048]{1,0:T(8,128)(2,1)S(1)} %collective-permute-done.16.refs_4_, ...), custom_call_target="tpu_custom_call" | custom-call | tf_op jit(solution)/shard_map/scores/pallas_call | solution.py:69
  137.1 3.4 %collective-permute-done.19 = f32[60,128]{1,0:T(8,128)S(1)} collective-permute-done((f32[60,128]{1,0:T(8,128)S(1)}, f32[60,128]{1,0:T(8,128)S(1)}, u32[]{:S(2)}, u32[]{:S(2)}) %collective-permute-start.19) | collective-permute-done | bytes 30752 | tf_op jit(solution)/shard_map/ppermute | solution.py:377
  140.6 6.1 %deltas.7 = (bf16[64,2048]{1,0:T(8,128)(2,1)S(1)}, bf16[72,2048]{1,0:T(8,128)(2,1)S(1)}, bf16[64,2048]{1,0:T(8,128)(2,1)S(1)}, bf16[72,2048]{1,0:T(8,128)(2,1)S(1)}, bf16[208,2048]{1,0:T(8,128)(2,1)S(1)}) custom-call(s32[64,1]{1,0:T(8,128)S(1)} %copy-done.7, s32[72,1]{1,0:T(8,128)S(1)} %copy-done.5, s32[64,1]{1,0:T(8,128)S(1)} %copy-done.8, ...), custom_call_target="tpu_custom_call" | custom-call | tf_op jit(solution)/shard_map/deltas/pallas_call | solution.py:111
  146.7 2.1 collective-permute-start.30
  148.8 4.3 %scores.8 = f32[16,128]{1,0:T(8,128)S(1)} custom-call(s32[64,1]{1,0:T(8,128)S(1)} %copy-done.1, s32[64,1]{1,0:T(8,128)S(1)} %copy-done.2, bf16[64,2048]{1,0:T(8,128)(2,1)} %collective-permute-done.20.refs_2_, bf16[64,2048]{1,0:T(8,128)(2,1)} %collective-permute-done.21.refs_3_, bf16[1024,2048]{1,0:T(8,128)(2,1)S(1)} %bitcast.71), custom_call_target="tpu_custom_call" | custom-call | tf_op jit(solution)/shard_map/scores/pallas_call | solution.py:69
  154.9 3.1 %collective-permute-done.23 = f32[16,128]{1,0:T(8,128)S(1)} collective-permute-done((f32[16,128]{1,0:T(8,128)S(1)}, f32[16,128]{1,0:T(8,128)S(1)}, u32[]{:S(2)}, u32[]{:S(2)}) %collective-permute-start.23) | collective-permute-done | bytes 8224 | tf_op jit(solution)/shard_map/ppermute | solution.py:377
  158.0 2.7 %deltas.8 = (bf16[64,2048]{1,0:T(8,128)(2,1)S(1)}, bf16[64,2048]{1,0:T(8,128)(2,1)S(1)}) custom-call(s32[64,1]{1,0:T(8,128)S(1)} %copy-done.1, s32[64,1]{1,0:T(8,128)S(1)} %copy-done.2, f32[16,128]{1,0:T(8,128)S(1)} %add.251.refs_2_, bf16[1024,2048]{1,0:T(8,128)(2,1)S(1)} %bitcast.75), custom_call_target="tpu_custom_call" | custom-call | tf_op jit(solution)/shard_map/deltas/pallas_call | solution.py:111
  160.8 2.0 collective-permute-start.24
  162.8 11.5 %collective-permute-done.26 = bf16[64,2048]{1,0:T(8,128)(2,1)S(1)} collective-permute-done((bf16[64,2048]{1,0:T(8,128)(2,1)S(1)}, bf16[64,2048]{1,0:T(8,128)(2,1)S(1)}, u32[]{:S(2)}, u32[]{:S(2)}) %collective-permute-start.26) | collective-permute-done | bytes 262176 | tf_op jit(solution)/shard_map/ppermute | solution.py:377
  174.4 2.5 %collective-permute-start.27 = (bf16[64,2048]{1,0:T(8,128)(2,1)S(1)}, bf16[64,2048]{1,0:T(8,128)(2,1)}, u32[]{:S(2)}, u32[]{:S(2)}) collective-permute-start(bf16[64,2048]{1,0:T(8,128)(2,1)S(1)} %add.253), channel_id=1, source_target_pairs={{0,12},{4,8},{8,4},{12,0},{1,13},{5,9},{9,5},{13,1},{2,14},{6,10},... | collective-permute-start | bytes 786440 | tf_op jit(solution)/shard_map/ppermute | solution.py:377
  178.4 2.2 collective-permute-done.11
  181.6 2.5 %collective-permute-start.29 = (bf16[72,2048]{1,0:T(8,128)(2,1)S(1)}, bf16[72,2048]{1,0:T(8,128)(2,1)}, u32[]{:S(2)}, u32[]{:S(2)}) collective-permute-start(bf16[72,2048]{1,0:T(8,128)(2,1)S(1)} %get-tuple-element.425), channel_id=1, source_target_pairs={{0,12},{4,8},{8,4},{12,0},{1,13},{5,9},{9,5},{13,1},{2,14},{6,10},... | collective-permute-start | bytes 884744 | tf_op jit(solution)/shard_map/ppermute | solution.py:377
  184.8 3.3 %collective-permute-done.27 = bf16[64,2048]{1,0:T(8,128)(2,1)} collective-permute-done((bf16[64,2048]{1,0:T(8,128)(2,1)S(1)}, bf16[64,2048]{1,0:T(8,128)(2,1)}, u32[]{:S(2)}, u32[]{:S(2)}) %collective-permute-start.27) | collective-permute-done | bytes 262176 | tf_op jit(solution)/shard_map/ppermute | solution.py:377
  188.2 18.5 %collective-permute-start.25 = (bf16[64,2048]{1,0:T(8,128)(2,1)}, bf16[64,2048]{1,0:T(8,128)(2,1)}, u32[]{:S(2)}, u32[]{:S(2)}) collective-permute-start(bf16[64,2048]{1,0:T(8,128)(2,1)} %add.252), channel_id=1, source_target_pairs={{0,8},{4,12},{8,0},{12,4},{1,9},{5,13},{9,1},{13,5},{2,10},{6,14},... | collective-permute-start | bytes 786440 | tf_op jit(solution)/shard_map/ppermute | solution.py:377
  207.9 16.1 %collective-permute-done.25 = bf16[64,2048]{1,0:T(8,128)(2,1)} collective-permute-done((bf16[64,2048]{1,0:T(8,128)(2,1)}, bf16[64,2048]{1,0:T(8,128)(2,1)}, u32[]{:S(2)}, u32[]{:S(2)}) %collective-permute-start.25) | collective-permute-done | bytes 262176 | tf_op jit(solution)/shard_map/ppermute | solution.py:377
  223.9 6.7 %conditional.1 = (bf16[4,128,2048]{2,1,0:T(8,128)(2,1)S(1)}) conditional(s32[]{:T(128)} %convert_element_type.24, (s32[512,1]{1,0:T(8,128)}, s32[1,64]{1,0:T(1,128)}, s32[1,64]{1,0:T(1,128)}, s32[1,72]{1,0:T(1,128)}, s32[1,72]{1,0:T(1,128)}, /*index=5*/s32[1,208]{1,0:T(1,128)S(1)}, bf16[64,2048]{1,0:T(8,128)(2,1)}, bf16[64,2048]{1,0:T(8,128)(2,1)}, ...), branch_computations={%region_0.0_spmd, %region_1.12_spmd} | conditional | flops 809101184 | bytes 60511864 | solution.py:479
  224.0 6.5 %finish.2 = bf16[512,2048]{1,0:T(8,128)(2,1)S(1)} custom-call(s32[512,1]{1,0:T(8,128)} %get-tuple-element.299.row_ref, s32[1,64]{1,0:T(1,128)} %get-tuple-element.300.refs_0_, s32[1,64]{1,0:T(1,128)} %get-tuple-element.301.refs_1_, s32[1,72]{1,0:T(1,128)} %get-tuple-element.302.refs_2_, s32[1,72]{1,0:T(1,128)} %get-tuple-element.303.refs_3_, ...), custom_call_target="tpu_custom_call" | custom-call | tf_op jit(solution)/shard_map/cond/branch_0_fun/finish/pallas_call | solution.py:141
  (78 shorter events, 16.2 us)
Async XLA Ops:
  6.6 89.5 %copy-start.40 = (s32[2,32]{1,0:T(2,128)}, s32[2,32]{1,0:T(2,128)S(1)}, u32[]{:S(2)}) copy-start(s32[2,32]{1,0:T(2,128)S(1)} %get-tuple-element.396.refs_0_) | copy-start | bytes 772
  13.8 7.8 %collective-permute-start.31 = (bf16[512,2048]{1,0:T(8,128)(2,1)S(1)}, bf16[512,2048]{1,0:T(8,128)(2,1)S(1)}, u32[]{:S(2)}, u32[]{:S(2)}) collective-permute-start(bf16[512,2048]{1,0:T(8,128)(2,1)S(1)} %share.6), channel_id=1, source_target_pairs={{0,1},{1,0},{2,3},{3,2},{4,5},{5,4},{6,7},{7,6},{8,9},{9,8},{10,11... | collective-permute-start | bytes 6291464 | tf_op jit(solution)/shard_map/ppermute | solution.py:377
  21.4 98.8 %collective-permute-start.12 = (bf16[512,2048]{1,0:T(8,128)(2,1)S(1)}, bf16[512,2048]{1,0:T(8,128)(2,1)}, u32[]{:S(2)}, u32[]{:S(2)}) collective-permute-start(bf16[512,2048]{1,0:T(8,128)(2,1)S(1)} %share.4), channel_id=1, source_target_pairs={{0,1},{1,0},{2,3},{3,2},{4,5},{5,4},{6,7},{7,6},{8,9},{9,8},{10,11... | collective-permute-start | bytes 6291464 | tf_op jit(solution)/shard_map/ppermute | solution.py:377
  29.7 194.2 %collective-permute-start.32 = (bf16[512,2048]{1,0:T(8,128)(2,1)}, bf16[512,2048]{1,0:T(8,128)(2,1)}, u32[]{:S(2)}, u32[]{:S(2)}) collective-permute-start(bf16[512,2048]{1,0:T(8,128)(2,1)} %share.7), channel_id=1, source_target_pairs={{0,2},{1,3},{2,0},{3,1},{4,6},{5,7},{6,4},{7,5},{8,10},{9,11},{10,... | collective-permute-start | bytes 6291464 | tf_op jit(solution)/shard_map/ppermute | solution.py:377
  32.7 96.0 %collective-permute-start.17 = (bf16[208,2048]{1,0:T(8,128)(2,1)}, bf16[208,2048]{1,0:T(8,128)(2,1)}, u32[]{:S(2)}, u32[]{:S(2)}) collective-permute-start(bf16[208,2048]{1,0:T(8,128)(2,1)} %get-tuple-element.417), channel_id=1, source_target_pairs={{0,4},{4,0},{8,12},{12,8},{1,5},{5,1},{9,13},{13,9},{2,6},{6,2},{1... | collective-permute-start | bytes 2555912 | tf_op jit(solution)/shard_map/ppermute | solution.py:377
  34.2 21.3 %collective-permute-start.10 = (s32[2,32]{1,0:T(2,128)S(1)}, s32[2,32]{1,0:T(2,128)S(1)}, u32[]{:S(2)}, u32[]{:S(2)}) collective-permute-start(s32[2,32]{1,0:T(2,128)S(1)} %get-tuple-element.396.refs_0_), channel_id=1, source_target_pairs={{0,12},{4,8},{8,4},{12,0},{1,13},{5,9},{9,5},{13,1},{2,14},{6,10},... | collective-permute-start | bytes 776 | tf_op jit(solution)/shard_map/ppermute | solution.py:377
  41.9 18.2 %collective-permute-start.13 = (f32[64,128]{1,0:T(8,128)S(1)}, f32[64,128]{1,0:T(8,128)S(1)}, u32[]{:S(2)}, u32[]{:S(2)}) collective-permute-start(f32[64,128]{1,0:T(8,128)S(1)} %scores.6), channel_id=1, source_target_pairs={{0,1},{1,0},{2,3},{3,2},{4,5},{5,4},{6,7},{7,6},{8,9},{9,8},{10,11... | collective-permute-start | bytes 98312 | tf_op jit(solution)/shard_map/ppermute | solution.py:377
  55.5 4.6 %collective-permute-start.9 = (s32[2,32]{1,0:T(2,128)S(1)}, s32[2,32]{1,0:T(2,128)S(1)}, u32[]{:S(2)}, u32[]{:S(2)}) collective-permute-start(s32[2,32]{1,0:T(2,128)S(1)} %get-tuple-element.396.refs_0_), channel_id=1, source_target_pairs={{0,8},{4,12},{8,0},{12,4},{1,9},{5,13},{9,1},{13,5},{2,10},{6,14},... | collective-permute-start | bytes 776 | tf_op jit(solution)/shard_map/ppermute | solution.py:377
  60.1 35.4 %collective-permute-start.15 = (bf16[136,2048]{1,0:T(8,128)(2,1)S(1)}, bf16[136,2048]{1,0:T(8,128)(2,1)S(1)}, u32[]{:S(2)}, u32[]{:S(2)}) collective-permute-start(bf16[136,2048]{1,0:T(8,128)(2,1)S(1)} %get-tuple-element.415), channel_id=1, source_target_pairs={{0,8},{4,12},{8,0},{12,4},{1,9},{5,13},{9,1},{13,5},{2,10},{6,14},... | collective-permute-start | bytes 1671176 | tf_op jit(solution)/shard_map/ppermute | solution.py:377
  60.1 35.9 %collective-permute-start.16 = (bf16[136,2048]{1,0:T(8,128)(2,1)S(1)}, bf16[136,2048]{1,0:T(8,128)(2,1)S(1)}, u32[]{:S(2)}, u32[]{:S(2)}) collective-permute-start(bf16[136,2048]{1,0:T(8,128)(2,1)S(1)} %get-tuple-element.416), channel_id=1, source_target_pairs={{0,12},{4,8},{8,4},{12,0},{1,13},{5,9},{9,5},{13,1},{2,14},{6,10},... | collective-permute-start | bytes 1671176 | tf_op jit(solution)/shard_map/ppermute | solution.py:377
  95.5 16.0 %collective-permute-start.14 = (f32[64,128]{1,0:T(8,128)S(1)}, f32[64,128]{1,0:T(8,128)S(1)}, u32[]{:S(2)}, u32[]{:S(2)}) collective-permute-start(f32[64,128]{1,0:T(8,128)S(1)} %add.246), channel_id=1, source_target_pairs={{0,2},{1,3},{2,0},{3,1},{4,6},{5,7},{6,4},{7,5},{8,10},{9,11},{10,... | collective-permute-start | bytes 98312 | tf_op jit(solution)/shard_map/ppermute | solution.py:377
  96.1 13.4 %collective-permute-start.8 = (s32[2,32]{1,0:T(2,128)S(1)}, s32[2,32]{1,0:T(2,128)S(1)}, u32[]{:S(2)}, u32[]{:S(2)}) collective-permute-start(s32[2,32]{1,0:T(2,128)S(1)} %get-tuple-element.396.refs_0_), channel_id=1, source_target_pairs={{0,4},{4,0},{8,12},{12,8},{1,5},{5,1},{9,13},{13,9},{2,6},{6,2},{1... | collective-permute-start | bytes 776 | tf_op jit(solution)/shard_map/ppermute | solution.py:377
  109.5 39.3 %collective-permute-start.20 = (bf16[64,2048]{1,0:T(8,128)(2,1)}, bf16[64,2048]{1,0:T(8,128)(2,1)}, u32[]{:S(2)}, u32[]{:S(2)}) collective-permute-start(bf16[64,2048]{1,0:T(8,128)(2,1)} %slice.32), channel_id=1, source_target_pairs={{0,4},{4,0},{8,12},{12,8},{1,5},{5,1},{9,13},{13,9},{2,6},{6,2},{1... | collective-permute-start | bytes 786440 | tf_op jit(solution)/shard_map/ppermute | solution.py:377
  111.5 37.2 %collective-permute-start.21 = (bf16[64,2048]{1,0:T(8,128)(2,1)}, bf16[64,2048]{1,0:T(8,128)(2,1)}, u32[]{:S(2)}, u32[]{:S(2)}) collective-permute-start(bf16[64,2048]{1,0:T(8,128)(2,1)} %slice.33), channel_id=1, source_target_pairs={{0,4},{4,0},{8,12},{12,8},{1,5},{5,1},{9,13},{13,9},{2,6},{6,2},{1... | collective-permute-start | bytes 786440 | tf_op jit(solution)/shard_map/ppermute | solution.py:377
  128.8 11.8 %copy-start.5 = (s32[72,1]{1,0:T(8,128)S(1)}, s32[72,1]{1,0:T(8,128)}, u32[]{:S(2)}) copy-start(s32[72,1]{1,0:T(8,128)} %get-tuple-element.405.refs_1_) | copy-start | bytes 868
  128.8 11.8 %copy-start.6 = (s32[72,1]{1,0:T(8,128)S(1)}, s32[72,1]{1,0:T(8,128)}, u32[]{:S(2)}) copy-start(s32[72,1]{1,0:T(8,128)} %get-tuple-element.407.refs_3_) | copy-start | bytes 868
  128.8 11.8 %copy-start.7 = (s32[64,1]{1,0:T(8,128)S(1)}, s32[64,1]{1,0:T(8,128)}, u32[]{:S(2)}) copy-start(s32[64,1]{1,0:T(8,128)} %get-tuple-element.404.refs_0_) | copy-start | bytes 772
  128.8 11.8 %copy-start.8 = (s32[64,1]{1,0:T(8,128)S(1)}, s32[64,1]{1,0:T(8,128)}, u32[]{:S(2)}) copy-start(s32[64,1]{1,0:T(8,128)} %get-tuple-element.406.refs_2_) | copy-start | bytes 772
  128.8 11.8 %copy-start.14 = (bf16[64,16,2048]{2,1,0:T(8,128)(2,1)S(1)}, bf16[64,16,2048]{2,1,0:T(8,128)(2,1)}, u32[]{:S(2)}) copy-start(bf16[64,16,2048]{2,1,0:T(8,128)(2,1)} %param.14) | copy-start | bytes 12582916
  135.3 1.3 collective-permute-start.18
  136.6 3.9 %collective-permute-start.19 = (f32[60,128]{1,0:T(8,128)S(1)}, f32[60,128]{1,0:T(8,128)S(1)}, u32[]{:S(2)}, u32[]{:S(2)}) collective-permute-start(f32[60,128]{1,0:T(8,128)S(1)} %add.248), channel_id=1, source_target_pairs={{0,2},{1,3},{2,0},{3,1},{4,6},{5,7},{6,4},{7,5},{8,10},{9,11},{10,... | collective-permute-start | bytes 92168 | tf_op jit(solution)/shard_map/ppermute | solution.py:377
  146.7 77.2 %collective-permute-start.30 = (bf16[208,2048]{1,0:T(8,128)(2,1)S(1)}, bf16[208,2048]{1,0:T(8,128)(2,1)}, u32[]{:S(2)}, u32[]{:S(2)}) collective-permute-start(bf16[208,2048]{1,0:T(8,128)(2,1)S(1)} %get-tuple-element.426), channel_id=1, source_target_pairs={{0,4},{4,0},{8,12},{12,8},{1,5},{5,1},{9,13},{13,9},{2,6},{6,2},{1... | collective-permute-start | bytes 2555912 | tf_op jit(solution)/shard_map/ppermute | solution.py:377
  153.1 1.2 collective-permute-start.22
  154.4 3.7 %collective-permute-start.23 = (f32[16,128]{1,0:T(8,128)S(1)}, f32[16,128]{1,0:T(8,128)S(1)}, u32[]{:S(2)}, u32[]{:S(2)}) collective-permute-start(f32[16,128]{1,0:T(8,128)S(1)} %add.250), channel_id=1, source_target_pairs={{0,2},{1,3},{2,0},{3,1},{4,6},{5,7},{6,4},{7,5},{8,10},{9,11},{10,... | collective-permute-start | bytes 24584 | tf_op jit(solution)/shard_map/ppermute | solution.py:377
  158.0 65.9 %copy-start.12 = (bf16[4,128,2048]{2,1,0:T(8,128)(2,1)S(1)}, bf16[4,128,2048]{2,1,0:T(8,128)(2,1)}, u32[]{:S(2)}) copy-start(bf16[4,128,2048]{2,1,0:T(8,128)(2,1)} %param.11) | copy-start | bytes 6291460
  160.7 13.5 %collective-permute-start.26 = (bf16[64,2048]{1,0:T(8,128)(2,1)S(1)}, bf16[64,2048]{1,0:T(8,128)(2,1)S(1)}, u32[]{:S(2)}, u32[]{:S(2)}) collective-permute-start(bf16[64,2048]{1,0:T(8,128)(2,1)S(1)} %get-tuple-element.423), channel_id=1, source_target_pairs={{0,4},{4,0},{8,12},{12,8},{1,5},{5,1},{9,13},{13,9},{2,6},{6,2},{1... | collective-permute-start | bytes 786440 | tf_op jit(solution)/shard_map/ppermute | solution.py:377
  160.8 20.7 %collective-permute-start.24 = (bf16[64,2048]{1,0:T(8,128)(2,1)S(1)}, bf16[64,2048]{1,0:T(8,128)(2,1)S(1)}, u32[]{:S(2)}, u32[]{:S(2)}) collective-permute-start(bf16[64,2048]{1,0:T(8,128)(2,1)S(1)} %get-tuple-element.421), channel_id=1, source_target_pairs={{0,4},{4,0},{8,12},{12,8},{1,5},{5,1},{9,13},{13,9},{2,6},{6,2},{1... | collective-permute-start | bytes 786440 | tf_op jit(solution)/shard_map/ppermute | solution.py:377
  174.4 13.8 %collective-permute-start.27 = (bf16[64,2048]{1,0:T(8,128)(2,1)S(1)}, bf16[64,2048]{1,0:T(8,128)(2,1)}, u32[]{:S(2)}, u32[]{:S(2)}) collective-permute-start(bf16[64,2048]{1,0:T(8,128)(2,1)S(1)} %add.253), channel_id=1, source_target_pairs={{0,12},{4,8},{8,4},{12,0},{1,13},{5,9},{9,5},{13,1},{2,14},{6,10},... | collective-permute-start | bytes 786440 | tf_op jit(solution)/shard_map/ppermute | solution.py:377
  176.9 3.7 %collective-permute-start.11 = (s32[1,1]{1,0:T(1,128)}, s32[1,1]{1,0:T(1,128)}, u32[]{:S(2)}, u32[]{:S(2)}) collective-permute-start(s32[1,1]{1,0:T(1,128)} %get-tuple-element.397), channel_id=1, source_target_pairs={{0,16},{16,0},{1,17},{17,1},{2,18},{18,2},{3,19},{19,3},{4,20},{20... | collective-permute-start | bytes 20 | tf_op jit(solution)/shard_map/ppermute | solution.py:377
  180.6 43.3 %collective-permute-start.28 = (bf16[72,2048]{1,0:T(8,128)(2,1)S(1)}, bf16[72,2048]{1,0:T(8,128)(2,1)}, u32[]{:S(2)}, u32[]{:S(2)}) collective-permute-start(bf16[72,2048]{1,0:T(8,128)(2,1)S(1)} %get-tuple-element.424), channel_id=1, source_target_pairs={{0,8},{4,12},{8,0},{12,4},{1,9},{5,13},{9,1},{13,5},{2,10},{6,14},... | collective-permute-start | bytes 884744 | tf_op jit(solution)/shard_map/ppermute | solution.py:377
  181.6 42.3 %collective-permute-start.29 = (bf16[72,2048]{1,0:T(8,128)(2,1)S(1)}, bf16[72,2048]{1,0:T(8,128)(2,1)}, u32[]{:S(2)}, u32[]{:S(2)}) collective-permute-start(bf16[72,2048]{1,0:T(8,128)(2,1)S(1)} %get-tuple-element.425), channel_id=1, source_target_pairs={{0,12},{4,8},{8,4},{12,0},{1,13},{5,9},{9,5},{13,1},{2,14},{6,10},... | collective-permute-start | bytes 884744 | tf_op jit(solution)/shard_map/ppermute | solution.py:377
  188.2 35.7 %collective-permute-start.25 = (bf16[64,2048]{1,0:T(8,128)(2,1)}, bf16[64,2048]{1,0:T(8,128)(2,1)}, u32[]{:S(2)}, u32[]{:S(2)}) collective-permute-start(bf16[64,2048]{1,0:T(8,128)(2,1)} %add.252), channel_id=1, source_target_pairs={{0,8},{4,12},{8,0},{12,4},{1,9},{5,13},{9,1},{13,5},{2,10},{6,14},... | collective-permute-start | bytes 786440 | tf_op jit(solution)/shard_map/ppermute | solution.py:377
  (10 other events, 63.7 us)
